TPU v7x, 512 devices: a whole 4x8x8 slice. The times are simulated.
512 devices in a mesh: rep: 32 (over x, z_lo, core), fsdp: 16 (over y, z_hi).
Axes of the slice: x: 4, y: 8, z: 8 (z_hi: 2, z_lo: 4; z = z_hi * 4 + z_lo), core: 2. Of those that a mesh axis runs over, the one named last changes fastest.
Arguments:
- inputs: bfloat16 [32, 4096, 2304], P('rep', 'fsdp'), may hold values from -6 to 6
- cotangent: bfloat16 [32, 4096, 1024], P('rep', 'fsdp'), may hold values from -6 to 6
- params: float32 [32, 2304, 1024], P('rep', 'fsdp'), may hold values from -6 to 6
- moment: float32 [32, 2304, 1024], P('rep', 'fsdp'), may hold values from -1.2 to 1.2
- second: float32 [32, 2304, 1024], P('rep', 'fsdp'), may hold values from 0.02 to 0.5
- drift: bfloat16 [32, 2304, 1024], P('rep', 'fsdp'), may hold values from -12 to 12
- anchor: float32 [2304, 1024], P('fsdp', 'rep'), may hold values from -6 to 6
- momentum: float32 [2304, 1024], P('fsdp', 'rep'), may hold values from -6 to 6
Outputs:
- merged: float32 [32, 2304, 1024], P('rep', 'fsdp')
- keys: bfloat16 [32, 4096, 1024], P('rep', 'fsdp')
- anchor_new: float32 [2304, 1024], P('fsdp', 'rep')
- momentum_new: float32 [2304, 1024], P('fsdp', 'rep')
All inputs are finite; a program needn't handle non-finite values.
Results may differ from a plain program's by a relative error of at most 0.005.
Values may be sent and summed in bfloat16 or wider, within the bound.
No kernel may reach another device: no remote copies, remote signals or barrier semaphores. Data moves between devices by JAX's collectives and lax.ppermute only.
A program may use at most 64 MiB of HBM per device.

v0:
```python
import jax
import jax.numpy as jnp
from jax import lax
from jax.sharding import PartitionSpec as P

HEAD_DIM = 128


def norm_backward(projected, upstream):
    rows = projected.shape[0]
    heads_view = projected.reshape(rows, -1, HEAD_DIM)
    grads_view = upstream.reshape(rows, -1, HEAD_DIM)
    rms = jnp.sqrt(jnp.mean(heads_view * heads_view, axis=-1, keepdims=True) + 1e-06)
    normed = heads_view / rms
    inner = jnp.mean(grads_view * normed, axis=-1, keepdims=True)
    return (normed.reshape(rows, -1), ((grads_view - normed * inner) / rms).reshape(rows, -1))


def shards(inputs, cotangent, params, moment, second, drift, anchor, momentum):
    tokens_x = inputs[0]
    weights = params[0]
    weights16 = weights.astype(jnp.bfloat16)
    projected = jnp.dot(
        tokens_x,
        lax.all_gather(weights16, "fsdp", axis=0, tiled=True),
        preferred_element_type=jnp.float32,
    )
    normed, slopes = norm_backward(projected, cotangent[0].astype(jnp.float32))
    keys = normed.astype(jnp.bfloat16)
    slopes = slopes.astype(jnp.bfloat16)
    feature_cols = lax.all_to_all(tokens_x, "fsdp", split_axis=1, concat_axis=0, tiled=True)
    gradient = lax.dot_general(
        feature_cols,
        lax.all_gather(slopes, "fsdp", axis=0, tiled=True),
        (((0,), (0,)), ((), ())),
        preferred_element_type=jnp.float32,
    )
    moment_one = 0.9 * moment[0] + 0.1 * gradient
    moment_two = 0.95 * second[0] + 0.05 * gradient * gradient
    stepped = weights - 0.4 * (moment_one / (jnp.sqrt(moment_two) + 1e-08) + 0.01 * weights)
    replicas = lax.axis_size("rep")
    drift_full = drift[0].astype(jnp.float32)
    anchor_full, momentum_full = (
        lax.all_gather(anchor, "rep", axis=1, tiled=True),
        lax.all_gather(momentum, "rep", axis=1, tiled=True),
    )
    delta = lax.psum(drift_full, "rep") / replicas
    momentum_wide = 0.9 * momentum_full + delta
    anchor_wide = anchor_full - 0.7 * (delta + 0.9 * momentum_wide)
    width = anchor.shape[1]
    offset = lax.axis_index("rep") * width
    anchor_new = lax.dynamic_slice_in_dim(anchor_wide, offset, width, 1)
    momentum_new = lax.dynamic_slice_in_dim(momentum_wide, offset, width, 1)
    merged = 0.3 * anchor_wide + 0.7 * stepped
    return (merged[None], keys[None], anchor_new, momentum_new)


def solution(mesh):
    return jax.shard_map(
        shards,
        mesh=mesh,
        in_specs=(
            P("rep", "fsdp", None),
            P("rep", "fsdp", None),
            P("rep", "fsdp", None),
            P("rep", "fsdp", None),
            P("rep", "fsdp", None),
            P("rep", "fsdp", None),
            P("fsdp", "rep"),
            P("fsdp", "rep"),
        ),
        out_specs=(
            P("rep", "fsdp", None),
            P("rep", "fsdp", None),
            P("fsdp", "rep"),
            P("fsdp", "rep"),
        ),
        check_vma=False,
    )
```

profile of v0, /device:TPU:32, one launch (start us, length us, event | category | flops | bytes accessed | tf_op | source)
XLA Modules:
  0.0 492.2 jit_solution(1234921417848492565)
XLA Ops:
  8.0 0.0 all-gather.3.cloned.1.call-start
  8.1 1.9 bitcast_convert_fusion
  9.9 0.0 all-gather.3.cloned.1.call-update
  10.0 0.0 all-reduce.2.cloned.1.call-start
  10.0 0.9 bitcast_convert_fusion.1
  10.9 0.0 all-reduce.2.cloned.1.call-update
  10.9 0.0 all-gather.5.cloned.1.call-start
  11.0 0.2 copy.30
  11.2 142.9 %all-gather.3.cloned.1.call-done = bf16[2304,1024]{1,0:T(8,128)(2,1)} async-done(((bf16[144,1024]{1,0:T(8,128)(2,1)}), bf16[2304,1024]{1,0:T(8,128)(2,1)}) %all-gather.3.cloned.1.call-update) | async-done | bytes 4718608 | tf_op jit(solution)/shard_map/all_gather | solution.py:25
  154.1 6.9 %copy.31 = bf16[1024,2304]{1,0:T(8,128)(2,1)} copy(bf16[1024,2304]{0,1:T(8,128)(2,1)} %bitcast.47) | data formatting | bytes 9437184 | tf_op jit(solution)/shard_map/dot_general | solution.py:23
  161.0 3.8 multiply_reduce_fusion.1
  164.8 0.2 multiply_reduce_fusion
  165.0 1.3 fusion.9
  166.3 0.0 all-gather.5.cloned.1.call-update
  166.4 1.5 copy.32
  167.8 7.4 %all-to-all-start = ((bf16[256,16,144]{0,2,1:T(8,128)(2,1)}), bf16[256,16,144]{0,2,1:T(8,128)(2,1)S(1)}, u32[]{:S(2)}, u32[]{:S(2)}) async-start(bf16[256,16,144]{0,2,1:T(8,128)(2,1)} %bitcast.9), calls=%async_computation | async-start | bytes 2359296 | tf_op jit(solution)/shard_map/all_to_all | solution.py:31
  175.2 0.0 copy-start.7
  175.2 72.7 %all_gather.12 = f32[144,1024]{0,1:T(8,128)S(1)} all-gather(f32[144,32]{0,1:T(8,128)S(1)} %copy-done.6), channel_id=1, replica_groups=mesh['rep'=32,'fsdp'=16] {'rep'}, dimensions={1}, use_global_device_ids=true | all-gather | bytes 608256 | tf_op jit(solution)/shard_map/all_gather | solution.py:44
  247.9 0.3 copy.29
  248.2 101.7 %all_gather.13 = f32[144,1024]{0,1:T(8,128)S(1)} all-gather(f32[144,32]{0,1:T(8,128)S(1)} %copy-done.7), channel_id=1, replica_groups=mesh['rep'=32,'fsdp'=16] {'rep'}, dimensions={1}, use_global_device_ids=true | all-gather | bytes 608256 | tf_op jit(solution)/shard_map/all_gather | solution.py:45
  349.9 0.3 copy.28
  350.2 121.8 %all-reduce.2.cloned.1.call-done = f32[144,1024]{1,0:T(8,128)} async-done(((f32[144,1024]{1,0:T(8,128)}), f32[144,1024]{1,0:T(8,128)}) %all-reduce.2.cloned.1.call-update) | async-done | bytes 589840 | tf_op jit(solution)/shard_map/psum | solution.py:47
  472.0 1.3 multiply_add_fusion
  473.2 0.0 copy-start.2
  473.3 0.1 constant_dynamic-slice_fusion
  473.4 0.7 copy.36
  474.1 0.7 copy.35
  474.8 0.0 all-to-all-done
  474.8 0.1 copy.37
  474.9 0.9 copy-done
  475.8 1.0 copy.34
  476.9 7.9 %add_bitcast_fusion = f32[1,144,1024]{2,1,0:T(8,128)} fusion(f32[1,144,1024]{2,1,0:T(8,128)} %param.12, f32[1,144,1024]{2,1,0:T(8,128)} %param.10, bf16[4096,1024]{0,1:T(8,128)(2,1)} %all-gather.5.cloned.1.call-done, bf16[4096,144]{0,1:T(8,128)(2,1)S(1)} %bitcast.52, f32[1,144,1024]{2,1,0:T(8,128)} %param.11, f32[144,1024]{1,0:T(8,128)S(1)} %copy-done.3), kind=kOutput, calls=%fused_computation.17 | convolution fusion | flops 1210318848 | bytes 12517376 | tf_op jit(solution)/shard_map/dot_general | solution.py:32
  (16 shorter events, 0.0 us)
Async XLA Ops:
  8.0 2.0 copy-start.5
  8.0 3.0 copy-start.4
  8.0 146.1 %all-gather.3.cloned.1.call-start = ((), (), s32[]{:S(2)}) async-start(), calls=%async_computation.2 | async-start | bytes 5013504 | tf_op jit(solution)/shard_map/all_gather | solution.py:25
  10.0 462.0 %all-reduce.2.cloned.1.call-start = ((), (), s32[]{:S(2)}) async-start(), calls=%async_computation.1 | async-start | bytes 1179648 | tf_op jit(solution)/shard_map/psum | solution.py:47
  10.9 465.9 %all-gather.5.cloned.1.call-start = ((), (), s32[]{:S(2)}) async-start(), calls=%async_computation.3 | async-start | bytes 8912896 | tf_op jit(solution)/shard_map/all_gather | solution.py:34
  154.1 6.9 %copy-start.1 = (bf16[1,256,2304]{2,1,0:T(8,128)(2,1)S(1)}, bf16[1,256,2304]{2,1,0:T(8,128)(2,1)}, u32[]{:S(2)}) copy-start(bf16[1,256,2304]{2,1,0:T(8,128)(2,1)} %param.8) | copy-start | bytes 3538948
  167.8 7.4 %copy-start.6 = (f32[144,32]{0,1:T(8,128)S(1)}, f32[144,32]{0,1:T(8,128)}, u32[]{:S(2)}) copy-start(f32[144,32]{0,1:T(8,128)} %param.14) | copy-start | bytes 55300
  167.8 307.0 %all-to-all-start = ((bf16[256,16,144]{0,2,1:T(8,128)(2,1)}), bf16[256,16,144]{0,2,1:T(8,128)(2,1)S(1)}, u32[]{:S(2)}, u32[]{:S(2)}) async-start(bf16[256,16,144]{0,2,1:T(8,128)(2,1)} %bitcast.9), calls=%async_computation | async-start | bytes 2359296 | tf_op jit(solution)/shard_map/all_to_all | solution.py:31
  175.2 73.0 %copy-start.7 = (f32[144,32]{0,1:T(8,128)S(1)}, f32[144,32]{0,1:T(8,128)}, u32[]{:S(2)}) copy-start(f32[144,32]{0,1:T(8,128)} %param.15) | copy-start | bytes 55300
  473.2 1.6 copy-start.2
  474.8 1.0 copy-start
  474.8 2.0 copy-start.3
Sparse Core Ops, SparseCore 0:
  12.6 141.4 all-gather.2
  166.5 243.6 all-gather.4
Sparse Core Ops, SparseCore 1:
  13.9 458.0 all-reduce.1
where the time goes:
time: 493 us; the launch traced here: 492 us
  waiting for transfers between devices  265 us (54%)
  blocking collectives  174 us (35%)
  between operations  15.6 us (3%)
  local copies, waits for them, and re-layouts  12.7 us (3%)
  matrix products  11.7 us (2%)
  starting transfers between devices  7.48 us (2%)
  other arithmetic  5.54 us (1%)
    all_gather x1, waiting for transfers between devices, shards(): lax.all_gather(weights16, 'fsdp', axis=0, tiled=True)  143 us
    psum x1, waiting for transfers between devices, shards(): delta = lax.psum(drift_full, 'rep') / replicas  122 us
    all_gather x1, blocking collectives, shards(): lax.all_gather(momentum, 'rep', axis=1, tiled=True)  102 us
    all_gather x1, blocking collectives, shards(): lax.all_gather(anchor, 'rep', axis=1, tiled=True)  72.7 us
  transfers between devices with their start and end apart: 4, of which 2 were waited for; matrix products, arithmetic and copies ran while one was open for 4% of the time, Pallas kernels for 0%

commit v1 on v0

v1 whole, which is shorter than its diff:
```python
import jax
import jax.numpy as jnp
from jax import lax
from jax.experimental import pallas as pl
from jax.experimental.pallas import tpu as pltpu
from jax.sharding import PartitionSpec as P

HEAD_DIM = 128
ZS = 2
VMEM_LIMIT = 40 * 1024 * 1024
F32 = jnp.float32
BF16 = jnp.bfloat16


def spec(space):
    return pl.BlockSpec(memory_space=space)


def forward_body(ids, x_ref, cot_ref, *refs):
    chunks, (keys_ref, slopes_ref, w_ref) = refs[:-3], refs[-3:]
    rows = chunks[0].shape[0]
    for n, chunk in enumerate(chunks):
        at = pl.multiple_of(ids[n] * rows, 16)
        w_ref[pl.ds(at, rows), :] = chunk[...]
    wide = 2 * HEAD_DIM
    for col in range(0, w_ref.shape[1], wide):
        projected = jnp.dot(x_ref[...], w_ref[:, col : col + wide], preferred_element_type=F32)
        for head in range(0, wide, HEAD_DIM):
            p = projected[:, head : head + HEAD_DIM]
            inv = 1.0 / jnp.sqrt(jnp.mean(p * p, axis=-1, keepdims=True) + 1e-06)
            normed = p * inv
            g = cot_ref[:, col + head : col + head + HEAD_DIM].astype(F32)
            inner = jnp.mean(g * normed, axis=-1, keepdims=True)
            keys_ref[:, col + head : col + head + HEAD_DIM] = normed.astype(BF16)
            slopes_ref[:, col + head : col + head + HEAD_DIM] = ((g - normed * inner) * inv).astype(BF16)


def forward(ids, x, cot, chunks):
    out = jax.ShapeDtypeStruct(cot.shape, BF16)
    return pl.pallas_call(
        forward_body,
        out_shape=(out, out),
        in_specs=[spec(pltpu.SMEM)] + [spec(pltpu.VMEM)] * (2 + len(chunks)),
        out_specs=(spec(pltpu.VMEM), spec(pltpu.VMEM)),
        scratch_shapes=[pltpu.VMEM((x.shape[1], cot.shape[1]), BF16)],
        compiler_params=pltpu.CompilerParams(vmem_limit_bytes=VMEM_LIMIT),
        cost_estimate=pl.CostEstimate(flops=2 * x.shape[0] * x.shape[1] * cot.shape[1], bytes_accessed=7 << 20, transcendentals=0),
        name="forward",
    )(ids, x, cot, *chunks)


def partial_body(ids, xt_ref, slopes_ref, *outs):
    rows = outs[0].shape[0]
    for n, out in enumerate(outs):
        at = pl.multiple_of(ids[n] * rows, 16)
        out[...] = jnp.dot(xt_ref[pl.ds(at, rows), :], slopes_ref[...], preferred_element_type=F32).astype(BF16)


def partials(ids, xt, slopes, count, rows):
    out = jax.ShapeDtypeStruct((rows, slopes.shape[1]), BF16)
    return pl.pallas_call(
        partial_body,
        out_shape=(out,) * count,
        in_specs=[spec(pltpu.SMEM), spec(pltpu.VMEM), spec(pltpu.VMEM)],
        out_specs=(spec(pltpu.VMEM),) * count,
        compiler_params=pltpu.CompilerParams(vmem_limit_bytes=VMEM_LIMIT),
        cost_estimate=pl.CostEstimate(
            flops=2 * count * rows * slopes.size, bytes_accessed=(2 << 20) + count * rows * 2048, transcendentals=0
        ),
        name="partials",
    )(ids, xt, slopes)


def shards(inputs, cotangent, params, moment, second, drift, anchor, momentum):
    x, weights = inputs[0], params[0]
    rows = weights.shape[0]
    size = lax.axis_size("fsdp")
    ys = size // ZS
    index = lax.axis_index("fsdp").astype(jnp.int32)
    y, z = index // ZS, index % ZS
    half = ys // 2

    def step(value, dy, dz=0):
        pairs = [(a * ZS + b, ((a + dy) % ys) * ZS + (b + dz) % ZS) for a in range(ys) for b in range(ZS)]
        return lax.ppermute(value, "fsdp", pairs)

    def owner(dy, dz):
        return ((y + dy) % ys) * ZS + (z + dz) % ZS

    reps = lax.axis_size("rep")
    width = anchor.shape[1]
    sent = drift[0].T.reshape(reps, width, rows)
    drifts = lax.all_to_all(sent, "rep", split_axis=0, concat_axis=0, tiled=True)
    delta = jnp.sum(drifts.astype(F32), axis=0) / reps
    momentum_new = 0.9 * momentum.T + delta
    anchor_new = anchor.T - 0.7 * (delta + 0.9 * momentum_new)
    copies = jnp.broadcast_to(anchor_new.astype(BF16)[None], (reps, width, rows))
    anchors = lax.all_to_all(copies, "rep", split_axis=0, concat_axis=0, tiled=True)
    anchor_wide = anchors.reshape(reps * width, rows).T.astype(F32)

    own = weights.astype(BF16)
    other = step(own, 0, 1)
    chunks, where = [own, other], [owner(0, 0), owner(0, 1)]
    for dz, first, last in ((0, own, 1), (1, other, -1)):
        for way in (1, -1):
            held = first
            for hop in range(1, half + (way == last)):
                held = step(held, way)
                chunks.append(held)
                where.append(owner(-way * hop, dz))
    keys, slopes = forward(jnp.stack(where), x, cotangent[0], chunks)

    xt = x.T
    far = partials(jnp.stack([owner(half, 1), owner(half, 0)]), xt, slopes, 2, rows)
    order = [(0, 0), (0, 1)] + [(s * hop, dz) for hop in range(1, half) for s in (1, -1) for dz in (1, 0)]
    parts = partials(jnp.stack([owner(*o) for o in order]), xt, slopes, len(order), rows)
    part = dict(zip(order, parts))
    sums = {}
    for dz, first, last in ((1, far[0], -1), (0, far[1], 1)):
        total = part[0, dz].astype(F32)
        for way in (1, -1):
            held = step(first, way) if way == last else None
            for hop in range(half - 1, 0, -1):
                mine = part[way * hop, dz]
                if held is not None:
                    mine = (mine.astype(F32) + held.astype(F32)).astype(BF16)
                held = step(mine, way)
            total = total + held.astype(F32)
        sums[dz] = total
    gradient = sums[0] + step(sums[1].astype(BF16), 0, 1).astype(F32)

    moment_one = 0.9 * moment[0] + 0.1 * gradient
    moment_two = 0.95 * second[0] + 0.05 * gradient * gradient
    stepped = weights - 0.4 * (moment_one / (jnp.sqrt(moment_two) + 1e-08) + 0.01 * weights)
    merged = 0.3 * anchor_wide + 0.7 * stepped
    return (merged[None], keys[None], anchor_new.T, momentum_new.T)


def solution(mesh):
    return jax.shard_map(
        shards,
        mesh=mesh,
        in_specs=(
            P("rep", "fsdp", None),
            P("rep", "fsdp", None),
            P("rep", "fsdp", None),
            P("rep", "fsdp", None),
            P("rep", "fsdp", None),
            P("rep", "fsdp", None),
            P("fsdp", "rep"),
            P("fsdp", "rep"),
        ),
        out_specs=(
            P("rep", "fsdp", None),
            P("rep", "fsdp", None),
            P("fsdp", "rep"),
            P("fsdp", "rep"),
        ),
        check_vma=False,
    )
```

time: 493 us -> 185 us (0.38)
  the two profiles are of different devices: /device:TPU:32 before, /device:TPU:64 now
where the time goes in v1:
time: 185 us; the launch traced here: 184 us
  starting transfers between devices  126 us (68%)
  waiting for transfers between devices  26.5 us (14%)
  local copies, waits for them, and re-layouts  11 us (6%)
  other arithmetic  10.9 us (6%)
  Pallas kernels  7.36 us (4%)
    ppermute x30, starting transfers between devices, step(): return lax.ppermute(value, 'fsdp', pairs)  112 us
    ppermute x30, waiting for transfers between devices, step(): return lax.ppermute(value, 'fsdp', pairs)  26.5 us
    unnamed x36, local copies, waits for them, and re-layouts  9.67 us
    all_to_all x1, starting transfers between devices, shards(): lax.all_to_all(copies, 'rep', split_axis=0, concat_axis=0, tiled=True)  7.74 us
    all_to_all x1, starting transfers between devices, shards(): lax.all_to_all(sent, 'rep', split_axis=0, concat_axis=0, tiled=True)  6.75 us
    pallas_call x1, Pallas kernels, forward(): pl.pallas_call(forward_body, out_shape=(out, out), in_specs=[spec(pltpu.S...  4.71 us
  transfers between devices with their start and end apart: 32, of which 6 were waited for; matrix products, arithmetic and copies ran while one was open for 6% of the time, Pallas kernels for 1%

profile of v1, /device:TPU:64, one launch (start us, length us, event | category | flops | bytes accessed | tf_op | source)
XLA Modules:
  0.0 183.6 jit_solution(15544730248018687761)
XLA Ops:
  1.7 10.1 %collective-permute-start = (bf16[144,1024]{1,0:T(8,128)(2,1)S(1)}, bf16[144,1024]{1,0:T(8,128)(2,1)S(1)}, u32[]{:S(2)}, u32[]{:S(2)}) collective-permute-start(bf16[144,1024]{1,0:T(8,128)(2,1)S(1)} %bitcast_convert_fusion.refs_0_), channel_id=1, source_target_pairs={{0,1},{1,0},{2,3},{3,2},{4,5},{5,4},{6,7},{7,6},{8,9},{9,8},{10,11... | collective-permute-start | bytes 884744 | tf_op jit(solution)/shard_map/ppermute | solution.py:85
  11.9 3.5 %collective-permute-start.1 = (bf16[144,1024]{1,0:T(8,128)(2,1)S(1)}, bf16[144,1024]{1,0:T(8,128)(2,1)S(1)}, u32[]{:S(2)}, u32[]{:S(2)}) collective-permute-start(bf16[144,1024]{1,0:T(8,128)(2,1)S(1)} %bitcast_convert_fusion.refs_0_), channel_id=1, source_target_pairs={{0,2},{1,3},{2,4},{3,5},{4,6},{5,7},{6,8},{7,9},{8,10},{9,11},{10,... | collective-permute-start | bytes 884744 | tf_op jit(solution)/shard_map/ppermute | solution.py:85
  15.4 10.0 %collective-permute-done.refs_1_ = bf16[144,1024]{1,0:T(8,128)(2,1)S(1)} collective-permute-done((bf16[144,1024]{1,0:T(8,128)(2,1)S(1)}, bf16[144,1024]{1,0:T(8,128)(2,1)S(1)}, u32[]{:S(2)}, u32[]{:S(2)}) %collective-permute-start) | collective-permute-done | bytes 294944 | tf_op jit(solution)/shard_map/ppermute | solution.py:85
  25.4 5.4 %collective-permute-start.11 = (bf16[144,1024]{1,0:T(8,128)(2,1)S(1)}, bf16[144,1024]{1,0:T(8,128)(2,1)S(1)}, u32[]{:S(2)}, u32[]{:S(2)}) collective-permute-start(bf16[144,1024]{1,0:T(8,128)(2,1)S(1)} %collective-permute-done.refs_1_), channel_id=1, source_target_pairs={{0,14},{1,15},{2,0},{3,1},{4,2},{5,3},{6,4},{7,5},{8,6},{9,7},{10,... | collective-permute-start | bytes 884744 | tf_op jit(solution)/shard_map/ppermute | solution.py:85
  30.7 3.3 %collective-permute-start.5 = (bf16[144,1024]{1,0:T(8,128)(2,1)S(1)}, bf16[144,1024]{1,0:T(8,128)(2,1)S(1)}, u32[]{:S(2)}, u32[]{:S(2)}) collective-permute-start(bf16[144,1024]{1,0:T(8,128)(2,1)S(1)} %bitcast_convert_fusion.refs_0_), channel_id=1, source_target_pairs={{0,14},{1,15},{2,0},{3,1},{4,2},{5,3},{6,4},{7,5},{8,6},{9,7},{10,... | collective-permute-start | bytes 884744 | tf_op jit(solution)/shard_map/ppermute | solution.py:85
  34.0 2.6 %collective-permute-start.8 = (bf16[144,1024]{1,0:T(8,128)(2,1)S(1)}, bf16[144,1024]{1,0:T(8,128)(2,1)S(1)}, u32[]{:S(2)}, u32[]{:S(2)}) collective-permute-start(bf16[144,1024]{1,0:T(8,128)(2,1)S(1)} %collective-permute-done.refs_1_), channel_id=1, source_target_pairs={{0,2},{1,3},{2,4},{3,5},{4,6},{5,7},{6,8},{7,9},{8,10},{9,11},{10,... | collective-permute-start | bytes 884744 | tf_op jit(solution)/shard_map/ppermute | solution.py:85
  38.6 5.2 %collective-permute-start.12 = (bf16[144,1024]{1,0:T(8,128)(2,1)S(1)}, bf16[144,1024]{1,0:T(8,128)(2,1)}, u32[]{:S(2)}, u32[]{:S(2)}) collective-permute-start(bf16[144,1024]{1,0:T(8,128)(2,1)S(1)} %collective-permute-done.11.refs_12_), channel_id=1, source_target_pairs={{0,14},{1,15},{2,0},{3,1},{4,2},{5,3},{6,4},{7,5},{8,6},{9,7},{10,... | collective-permute-start | bytes 884744 | tf_op jit(solution)/shard_map/ppermute | solution.py:85
  43.8 2.0 %copy.15 = bf16[1,144,1024]{1,2,0:T(8,128)(2,1)} copy(bf16[1,144,1024]{2,1,0:T(8,128)(2,1)} %param.13) | data formatting | bytes 589824 | tf_op args[5]
  45.8 6.7 %all-to-all-start = ((bf16[32,32,144]{2,1,0:T(8,128)(2,1)}), bf16[32,32,144]{2,1,0:T(8,128)(2,1)}, u32[]{:S(2)}, u32[]{:S(2)}) async-start(bf16[32,32,144]{2,1,0:T(8,128)(2,1)} %bitcast.80), calls=%async_computation | async-start | bytes 1048576 | tf_op jit(solution)/shard_map/all_to_all | solution.py:93
  52.5 3.2 %collective-permute-start.6 = (bf16[144,1024]{1,0:T(8,128)(2,1)S(1)}, bf16[144,1024]{1,0:T(8,128)(2,1)}, u32[]{:S(2)}, u32[]{:S(2)}) collective-permute-start(bf16[144,1024]{1,0:T(8,128)(2,1)S(1)} %collective-permute-done.5.refs_6_), channel_id=1, source_target_pairs={{0,14},{1,15},{2,0},{3,1},{4,2},{5,3},{6,4},{7,5},{8,6},{9,7},{10,... | collective-permute-start | bytes 884744 | tf_op jit(solution)/shard_map/ppermute | solution.py:85
  55.8 2.6 %collective-permute-start.9 = (bf16[144,1024]{1,0:T(8,128)(2,1)S(1)}, bf16[144,1024]{1,0:T(8,128)(2,1)}, u32[]{:S(2)}, u32[]{:S(2)}) collective-permute-start(bf16[144,1024]{1,0:T(8,128)(2,1)S(1)} %collective-permute-done.8.refs_9_), channel_id=1, source_target_pairs={{0,2},{1,3},{2,4},{3,5},{4,6},{5,7},{6,8},{7,9},{8,10},{9,11},{10,... | collective-permute-start | bytes 884744 | tf_op jit(solution)/shard_map/ppermute | solution.py:85
  61.8 5.1 %collective-permute-start.13 = (bf16[144,1024]{1,0:T(8,128)(2,1)}, bf16[144,1024]{1,0:T(8,128)(2,1)}, u32[]{:S(2)}, u32[]{:S(2)}) collective-permute-start(bf16[144,1024]{1,0:T(8,128)(2,1)} %collective-permute-done.12.refs_13_), channel_id=1, source_target_pairs={{0,14},{1,15},{2,0},{3,1},{4,2},{5,3},{6,4},{7,5},{8,6},{9,7},{10,... | collective-permute-start | bytes 884744 | tf_op jit(solution)/shard_map/ppermute | solution.py:85
  66.9 3.2 %collective-permute-start.7 = (bf16[144,1024]{1,0:T(8,128)(2,1)}, bf16[144,1024]{1,0:T(8,128)(2,1)}, u32[]{:S(2)}, u32[]{:S(2)}) collective-permute-start(bf16[144,1024]{1,0:T(8,128)(2,1)} %collective-permute-done.6.refs_7_), channel_id=1, source_target_pairs={{0,14},{1,15},{2,0},{3,1},{4,2},{5,3},{6,4},{7,5},{8,6},{9,7},{10,... | collective-permute-start | bytes 884744 | tf_op jit(solution)/shard_map/ppermute | solution.py:85
  70.2 2.6 %collective-permute-start.10 = (bf16[144,1024]{1,0:T(8,128)(2,1)}, bf16[144,1024]{1,0:T(8,128)(2,1)}, u32[]{:S(2)}, u32[]{:S(2)}) collective-permute-start(bf16[144,1024]{1,0:T(8,128)(2,1)} %collective-permute-done.9.refs_10_), channel_id=1, source_target_pairs={{0,2},{1,3},{2,4},{3,5},{4,6},{5,7},{6,8},{7,9},{8,10},{9,11},{10,... | collective-permute-start | bytes 884744 | tf_op jit(solution)/shard_map/ppermute | solution.py:85
  76.0 5.1 %collective-permute-start.14 = (bf16[144,1024]{1,0:T(8,128)(2,1)}, bf16[144,1024]{1,0:T(8,128)(2,1)}, u32[]{:S(2)}, u32[]{:S(2)}) collective-permute-start(bf16[144,1024]{1,0:T(8,128)(2,1)} %collective-permute-done.13.refs_14_), channel_id=1, source_target_pairs={{0,14},{1,15},{2,0},{3,1},{4,2},{5,3},{6,4},{7,5},{8,6},{9,7},{10,... | collective-permute-start | bytes 884744 | tf_op jit(solution)/shard_map/ppermute | solution.py:85
  83.5 4.1 %collective-permute-done.4.refs_5_ = bf16[144,1024]{1,0:T(8,128)(2,1)} collective-permute-done((bf16[144,1024]{1,0:T(8,128)(2,1)}, bf16[144,1024]{1,0:T(8,128)(2,1)}, u32[]{:S(2)}, u32[]{:S(2)}) %collective-permute-start.4) | collective-permute-done | bytes 294944 | tf_op jit(solution)/shard_map/ppermute | solution.py:85
  92.4 4.7 %forward.1 = (bf16[256,1024]{1,0:T(8,128)(2,1)}, bf16[256,1024]{1,0:T(8,128)(2,1)S(1)}) custom-call(s32[16]{0:T(128)S(1)} %stack.92.ids, bf16[256,2304]{1,0:T(8,128)(2,1)S(1)} %bitcast.75, bf16[256,1024]{1,0:T(8,128)(2,1)S(1)} %bitcast.78, bf16[144,1024]{1,0:T(8,128)(2,1)S(1)} %bitcast_convert_fusion.refs_0_, ...), custom_call_target="tpu_custom_call" | custom-call | flops 1207959552 | bytes 7340032 | tf_op jit(solution)/shard_map/forward/pallas_call | solution.py:40
  98.8 2.0 %collective-permute-start.15 = (bf16[144,1024]{1,0:T(8,128)(2,1)S(1)}, bf16[144,1024]{1,0:T(8,128)(2,1)}, u32[]{:S(2)}, u32[]{:S(2)}) collective-permute-start(bf16[144,1024]{1,0:T(8,128)(2,1)S(1)} %get-tuple-element.27), channel_id=1, source_target_pairs={{0,2},{1,3},{2,4},{3,5},{4,6},{5,7},{6,8},{7,9},{8,10},{9,11},{10,... | collective-permute-start | bytes 884744 | tf_op jit(solution)/shard_map/ppermute | solution.py:85
  101.7 7.7 %all-to-all-start.1 = ((bf16[32,32,144]{2,1,0:T(8,128)(2,1)}), bf16[32,32,144]{2,1,0:T(8,128)(2,1)}, u32[]{:S(2)}, u32[]{:S(2)}) async-start(bf16[32,32,144]{2,1,0:T(8,128)(2,1)} %broadcast_in_dim.12), calls=%async_computation.1 | async-start | bytes 1048576 | tf_op jit(solution)/shard_map/all_to_all | solution.py:98
  109.5 5.1 %collective-permute-start.25 = (bf16[144,1024]{1,0:T(8,128)(2,1)S(1)}, bf16[144,1024]{1,0:T(8,128)(2,1)S(1)}, u32[]{:S(2)}, u32[]{:S(2)}) collective-permute-start(bf16[144,1024]{1,0:T(8,128)(2,1)S(1)} %get-tuple-element.38), channel_id=1, source_target_pairs={{0,14},{1,15},{2,0},{3,1},{4,2},{5,3},{6,4},{7,5},{8,6},{9,7},{10,... | collective-permute-start | bytes 884744 | tf_op jit(solution)/shard_map/ppermute | solution.py:85
  116.4 3.4 %collective-permute-start.19 = (bf16[144,1024]{1,0:T(8,128)(2,1)S(1)}, bf16[144,1024]{1,0:T(8,128)(2,1)S(1)}, u32[]{:S(2)}, u32[]{:S(2)}) collective-permute-start(bf16[144,1024]{1,0:T(8,128)(2,1)S(1)} %get-tuple-element.30), channel_id=1, source_target_pairs={{0,14},{1,15},{2,0},{3,1},{4,2},{5,3},{6,4},{7,5},{8,6},{9,7},{10,... | collective-permute-start | bytes 884744 | tf_op jit(solution)/shard_map/ppermute | solution.py:85
  119.9 2.4 %collective-permute-start.22 = (bf16[144,1024]{1,0:T(8,128)(2,1)S(1)}, bf16[144,1024]{1,0:T(8,128)(2,1)S(1)}, u32[]{:S(2)}, u32[]{:S(2)}) collective-permute-start(bf16[144,1024]{1,0:T(8,128)(2,1)S(1)} %get-tuple-element.34), channel_id=1, source_target_pairs={{0,2},{1,3},{2,4},{3,5},{4,6},{5,7},{6,8},{7,9},{8,10},{9,11},{10,... | collective-permute-start | bytes 884744 | tf_op jit(solution)/shard_map/ppermute | solution.py:85
  125.4 5.1 %collective-permute-start.26 = (bf16[144,1024]{1,0:T(8,128)(2,1)S(1)}, bf16[144,1024]{1,0:T(8,128)(2,1)S(1)}, u32[]{:S(2)}, u32[]{:S(2)}) collective-permute-start(bf16[144,1024]{1,0:T(8,128)(2,1)S(1)} %add_convert_fusion.3), channel_id=1, source_target_pairs={{0,14},{1,15},{2,0},{3,1},{4,2},{5,3},{6,4},{7,5},{8,6},{9,7},{10,... | collective-permute-start | bytes 884744 | tf_op jit(solution)/shard_map/ppermute | solution.py:85
  130.6 3.4 %collective-permute-start.20 = (bf16[144,1024]{1,0:T(8,128)(2,1)S(1)}, bf16[144,1024]{1,0:T(8,128)(2,1)S(1)}, u32[]{:S(2)}, u32[]{:S(2)}) collective-permute-start(bf16[144,1024]{1,0:T(8,128)(2,1)S(1)} %add_convert_fusion.7), channel_id=1, source_target_pairs={{0,14},{1,15},{2,0},{3,1},{4,2},{5,3},{6,4},{7,5},{8,6},{9,7},{10,... | collective-permute-start | bytes 884744 | tf_op jit(solution)/shard_map/ppermute | solution.py:85
  134.2 2.4 %collective-permute-start.23 = (bf16[144,1024]{1,0:T(8,128)(2,1)S(1)}, bf16[144,1024]{1,0:T(8,128)(2,1)S(1)}, u32[]{:S(2)}, u32[]{:S(2)}) collective-permute-start(bf16[144,1024]{1,0:T(8,128)(2,1)S(1)} %add_convert_fusion.5), channel_id=1, source_target_pairs={{0,2},{1,3},{2,4},{3,5},{4,6},{5,7},{6,8},{7,9},{8,10},{9,11},{10,... | collective-permute-start | bytes 884744 | tf_op jit(solution)/shard_map/ppermute | solution.py:85
  138.1 5.6 %collective-permute-start.27 = (bf16[144,1024]{1,0:T(8,128)(2,1)S(1)}, bf16[144,1024]{1,0:T(8,128)(2,1)S(1)}, u32[]{:S(2)}, u32[]{:S(2)}) collective-permute-start(bf16[144,1024]{1,0:T(8,128)(2,1)S(1)} %add_convert_fusion.2), channel_id=1, source_target_pairs={{0,14},{1,15},{2,0},{3,1},{4,2},{5,3},{6,4},{7,5},{8,6},{9,7},{10,... | collective-permute-start | bytes 884744 | tf_op jit(solution)/shard_map/ppermute | solution.py:85
  148.7 5.6 %collective-permute-start.28 = (bf16[144,1024]{1,0:T(8,128)(2,1)S(1)}, bf16[144,1024]{1,0:T(8,128)(2,1)S(1)}, u32[]{:S(2)}, u32[]{:S(2)}) collective-permute-start(bf16[144,1024]{1,0:T(8,128)(2,1)S(1)} %add_convert_fusion.1), channel_id=1, source_target_pairs={{0,14},{1,15},{2,0},{3,1},{4,2},{5,3},{6,4},{7,5},{8,6},{9,7},{10,... | collective-permute-start | bytes 884744 | tf_op jit(solution)/shard_map/ppermute | solution.py:85
  155.1 2.6 %collective-permute-start.21 = (bf16[144,1024]{1,0:T(8,128)(2,1)}, bf16[144,1024]{1,0:T(8,128)(2,1)S(1)}, u32[]{:S(2)}, u32[]{:S(2)}) collective-permute-start(bf16[144,1024]{1,0:T(8,128)(2,1)} %add_convert_fusion.6), channel_id=1, source_target_pairs={{0,14},{1,15},{2,0},{3,1},{4,2},{5,3},{6,4},{7,5},{8,6},{9,7},{10,... | collective-permute-start | bytes 884744 | tf_op jit(solution)/shard_map/ppermute | solution.py:85
  158.5 3.3 %collective-permute-start.18 = (bf16[144,1024]{1,0:T(8,128)(2,1)}, bf16[144,1024]{1,0:T(8,128)(2,1)S(1)}, u32[]{:S(2)}, u32[]{:S(2)}) collective-permute-start(bf16[144,1024]{1,0:T(8,128)(2,1)} %add_convert_fusion.8), channel_id=1, source_target_pairs={{0,2},{1,3},{2,4},{3,5},{4,6},{5,7},{6,8},{7,9},{8,10},{9,11},{10,... | collective-permute-start | bytes 884744 | tf_op jit(solution)/shard_map/ppermute | solution.py:85
  162.6 7.3 %collective-permute-start.29 = (bf16[144,1024]{1,0:T(8,128)(2,1)}, bf16[144,1024]{1,0:T(8,128)(2,1)}, u32[]{:S(2)}, u32[]{:S(2)}) collective-permute-start(bf16[144,1024]{1,0:T(8,128)(2,1)} %add_convert_fusion), channel_id=1, source_target_pairs={{0,1},{1,0},{2,3},{3,2},{4,5},{5,4},{6,7},{7,6},{8,9},{9,8},{10,11... | collective-permute-start | bytes 884744 | tf_op jit(solution)/shard_map/ppermute | solution.py:85
  172.1 8.8 %collective-permute-done.29 = bf16[144,1024]{1,0:T(8,128)(2,1)} collective-permute-done((bf16[144,1024]{1,0:T(8,128)(2,1)}, bf16[144,1024]{1,0:T(8,128)(2,1)}, u32[]{:S(2)}, u32[]{:S(2)}) %collective-permute-start.29) | collective-permute-done | bytes 294944 | tf_op jit(solution)/shard_map/ppermute | solution.py:85
  180.8 2.7 %fusion.7 = f32[1,144,1024]{2,1,0:T(8,128)} fusion(f32[1024,144]{0,1:T(8,128)S(1)} %copy.16, f32[1,144,1024]{2,1,0:T(8,128)} %param.12, f32[1,144,1024]{2,1,0:T(8,128)S(1)} %copy-done.14, bf16[144,1024]{1,0:T(8,128)(2,1)} %collective-permute-done.29, bf16[144,1024]{1,0:T(8,128)(2,1)S(1)} %collective-permute-done.21, ...), kind=kLoop, calls=%fused_computation.14 | loop fusion | flops 3244032 | bytes 4128768 | tf_op jit(solution)/shard_map/broadcast_in_dim | solution.py:136
  (93 shorter events, 35.1 us)
Async XLA Ops:
  1.7 23.6 %collective-permute-start = (bf16[144,1024]{1,0:T(8,128)(2,1)S(1)}, bf16[144,1024]{1,0:T(8,128)(2,1)S(1)}, u32[]{:S(2)}, u32[]{:S(2)}) collective-permute-start(bf16[144,1024]{1,0:T(8,128)(2,1)S(1)} %bitcast_convert_fusion.refs_0_), channel_id=1, source_target_pairs={{0,1},{1,0},{2,3},{3,2},{4,5},{5,4},{6,7},{7,6},{8,9},{9,8},{10,11... | collective-permute-start | bytes 884744 | tf_op jit(solution)/shard_map/ppermute | solution.py:85
  11.9 24.7 %collective-permute-start.1 = (bf16[144,1024]{1,0:T(8,128)(2,1)S(1)}, bf16[144,1024]{1,0:T(8,128)(2,1)S(1)}, u32[]{:S(2)}, u32[]{:S(2)}) collective-permute-start(bf16[144,1024]{1,0:T(8,128)(2,1)S(1)} %bitcast_convert_fusion.refs_0_), channel_id=1, source_target_pairs={{0,2},{1,3},{2,4},{3,5},{4,6},{5,7},{6,8},{7,9},{8,10},{9,11},{10,... | collective-permute-start | bytes 884744 | tf_op jit(solution)/shard_map/ppermute | solution.py:85
  25.4 13.2 %collective-permute-start.11 = (bf16[144,1024]{1,0:T(8,128)(2,1)S(1)}, bf16[144,1024]{1,0:T(8,128)(2,1)S(1)}, u32[]{:S(2)}, u32[]{:S(2)}) collective-permute-start(bf16[144,1024]{1,0:T(8,128)(2,1)S(1)} %collective-permute-done.refs_1_), channel_id=1, source_target_pairs={{0,14},{1,15},{2,0},{3,1},{4,2},{5,3},{6,4},{7,5},{8,6},{9,7},{10,... | collective-permute-start | bytes 884744 | tf_op jit(solution)/shard_map/ppermute | solution.py:85
  30.7 21.8 %collective-permute-start.5 = (bf16[144,1024]{1,0:T(8,128)(2,1)S(1)}, bf16[144,1024]{1,0:T(8,128)(2,1)S(1)}, u32[]{:S(2)}, u32[]{:S(2)}) collective-permute-start(bf16[144,1024]{1,0:T(8,128)(2,1)S(1)} %bitcast_convert_fusion.refs_0_), channel_id=1, source_target_pairs={{0,14},{1,15},{2,0},{3,1},{4,2},{5,3},{6,4},{7,5},{8,6},{9,7},{10,... | collective-permute-start | bytes 884744 | tf_op jit(solution)/shard_map/ppermute | solution.py:85
  34.0 21.8 %collective-permute-start.8 = (bf16[144,1024]{1,0:T(8,128)(2,1)S(1)}, bf16[144,1024]{1,0:T(8,128)(2,1)S(1)}, u32[]{:S(2)}, u32[]{:S(2)}) collective-permute-start(bf16[144,1024]{1,0:T(8,128)(2,1)S(1)} %collective-permute-done.refs_1_), channel_id=1, source_target_pairs={{0,2},{1,3},{2,4},{3,5},{4,6},{5,7},{6,8},{7,9},{8,10},{9,11},{10,... | collective-permute-start | bytes 884744 | tf_op jit(solution)/shard_map/ppermute | solution.py:85
  36.6 22.5 %collective-permute-start.2 = (bf16[144,1024]{1,0:T(8,128)(2,1)S(1)}, bf16[144,1024]{1,0:T(8,128)(2,1)S(1)}, u32[]{:S(2)}, u32[]{:S(2)}) collective-permute-start(bf16[144,1024]{1,0:T(8,128)(2,1)S(1)} %collective-permute-done.1.refs_2_), channel_id=1, source_target_pairs={{0,2},{1,3},{2,4},{3,5},{4,6},{5,7},{6,8},{7,9},{8,10},{9,11},{10,... | collective-permute-start | bytes 884744 | tf_op jit(solution)/shard_map/ppermute | solution.py:85
  38.6 23.2 %collective-permute-start.12 = (bf16[144,1024]{1,0:T(8,128)(2,1)S(1)}, bf16[144,1024]{1,0:T(8,128)(2,1)}, u32[]{:S(2)}, u32[]{:S(2)}) collective-permute-start(bf16[144,1024]{1,0:T(8,128)(2,1)S(1)} %collective-permute-done.11.refs_12_), channel_id=1, source_target_pairs={{0,14},{1,15},{2,0},{3,1},{4,2},{5,3},{6,4},{7,5},{8,6},{9,7},{10,... | collective-permute-start | bytes 884744 | tf_op jit(solution)/shard_map/ppermute | solution.py:85
  45.8 36.6 %all-to-all-start = ((bf16[32,32,144]{2,1,0:T(8,128)(2,1)}), bf16[32,32,144]{2,1,0:T(8,128)(2,1)}, u32[]{:S(2)}, u32[]{:S(2)}) async-start(bf16[32,32,144]{2,1,0:T(8,128)(2,1)} %bitcast.80), calls=%async_computation | async-start | bytes 1048576 | tf_op jit(solution)/shard_map/all_to_all | solution.py:93
  52.5 14.4 %collective-permute-start.6 = (bf16[144,1024]{1,0:T(8,128)(2,1)S(1)}, bf16[144,1024]{1,0:T(8,128)(2,1)}, u32[]{:S(2)}, u32[]{:S(2)}) collective-permute-start(bf16[144,1024]{1,0:T(8,128)(2,1)S(1)} %collective-permute-done.5.refs_6_), channel_id=1, source_target_pairs={{0,14},{1,15},{2,0},{3,1},{4,2},{5,3},{6,4},{7,5},{8,6},{9,7},{10,... | collective-permute-start | bytes 884744 | tf_op jit(solution)/shard_map/ppermute | solution.py:85
  55.8 14.4 %collective-permute-start.9 = (bf16[144,1024]{1,0:T(8,128)(2,1)S(1)}, bf16[144,1024]{1,0:T(8,128)(2,1)}, u32[]{:S(2)}, u32[]{:S(2)}) collective-permute-start(bf16[144,1024]{1,0:T(8,128)(2,1)S(1)} %collective-permute-done.8.refs_9_), channel_id=1, source_target_pairs={{0,2},{1,3},{2,4},{3,5},{4,6},{5,7},{6,8},{7,9},{8,10},{9,11},{10,... | collective-permute-start | bytes 884744 | tf_op jit(solution)/shard_map/ppermute | solution.py:85
  59.1 15.0 %collective-permute-start.3 = (bf16[144,1024]{1,0:T(8,128)(2,1)S(1)}, bf16[144,1024]{1,0:T(8,128)(2,1)}, u32[]{:S(2)}, u32[]{:S(2)}) collective-permute-start(bf16[144,1024]{1,0:T(8,128)(2,1)S(1)} %collective-permute-done.2.refs_3_), channel_id=1, source_target_pairs={{0,2},{1,3},{2,4},{3,5},{4,6},{5,7},{6,8},{7,9},{8,10},{9,11},{10,... | collective-permute-start | bytes 884744 | tf_op jit(solution)/shard_map/ppermute | solution.py:85
  61.8 14.2 %collective-permute-start.13 = (bf16[144,1024]{1,0:T(8,128)(2,1)}, bf16[144,1024]{1,0:T(8,128)(2,1)}, u32[]{:S(2)}, u32[]{:S(2)}) collective-permute-start(bf16[144,1024]{1,0:T(8,128)(2,1)} %collective-permute-done.12.refs_13_), channel_id=1, source_target_pairs={{0,14},{1,15},{2,0},{3,1},{4,2},{5,3},{6,4},{7,5},{8,6},{9,7},{10,... | collective-permute-start | bytes 884744 | tf_op jit(solution)/shard_map/ppermute | solution.py:85
  66.9 16.6 %collective-permute-start.7 = (bf16[144,1024]{1,0:T(8,128)(2,1)}, bf16[144,1024]{1,0:T(8,128)(2,1)}, u32[]{:S(2)}, u32[]{:S(2)}) collective-permute-start(bf16[144,1024]{1,0:T(8,128)(2,1)} %collective-permute-done.6.refs_7_), channel_id=1, source_target_pairs={{0,14},{1,15},{2,0},{3,1},{4,2},{5,3},{6,4},{7,5},{8,6},{9,7},{10,... | collective-permute-start | bytes 884744 | tf_op jit(solution)/shard_map/ppermute | solution.py:85
  70.2 13.3 %collective-permute-start.10 = (bf16[144,1024]{1,0:T(8,128)(2,1)}, bf16[144,1024]{1,0:T(8,128)(2,1)}, u32[]{:S(2)}, u32[]{:S(2)}) collective-permute-start(bf16[144,1024]{1,0:T(8,128)(2,1)} %collective-permute-done.9.refs_10_), channel_id=1, source_target_pairs={{0,2},{1,3},{2,4},{3,5},{4,6},{5,7},{6,8},{7,9},{8,10},{9,11},{10,... | collective-permute-start | bytes 884744 | tf_op jit(solution)/shard_map/ppermute | solution.py:85
  74.1 13.5 %collective-permute-start.4 = (bf16[144,1024]{1,0:T(8,128)(2,1)}, bf16[144,1024]{1,0:T(8,128)(2,1)}, u32[]{:S(2)}, u32[]{:S(2)}) collective-permute-start(bf16[144,1024]{1,0:T(8,128)(2,1)} %collective-permute-done.3.refs_4_), channel_id=1, source_target_pairs={{0,2},{1,3},{2,4},{3,5},{4,6},{5,7},{6,8},{7,9},{8,10},{9,11},{10,... | collective-permute-start | bytes 884744 | tf_op jit(solution)/shard_map/ppermute | solution.py:85
  76.0 11.6 %collective-permute-start.14 = (bf16[144,1024]{1,0:T(8,128)(2,1)}, bf16[144,1024]{1,0:T(8,128)(2,1)}, u32[]{:S(2)}, u32[]{:S(2)}) collective-permute-start(bf16[144,1024]{1,0:T(8,128)(2,1)} %collective-permute-done.13.refs_14_), channel_id=1, source_target_pairs={{0,14},{1,15},{2,0},{3,1},{4,2},{5,3},{6,4},{7,5},{8,6},{9,7},{10,... | collective-permute-start | bytes 884744 | tf_op jit(solution)/shard_map/ppermute | solution.py:85
  98.8 23.5 %collective-permute-start.15 = (bf16[144,1024]{1,0:T(8,128)(2,1)S(1)}, bf16[144,1024]{1,0:T(8,128)(2,1)}, u32[]{:S(2)}, u32[]{:S(2)}) collective-permute-start(bf16[144,1024]{1,0:T(8,128)(2,1)S(1)} %get-tuple-element.27), channel_id=1, source_target_pairs={{0,2},{1,3},{2,4},{3,5},{4,6},{5,7},{6,8},{7,9},{8,10},{9,11},{10,... | collective-permute-start | bytes 884744 | tf_op jit(solution)/shard_map/ppermute | solution.py:85
  101.7 68.9 %all-to-all-start.1 = ((bf16[32,32,144]{2,1,0:T(8,128)(2,1)}), bf16[32,32,144]{2,1,0:T(8,128)(2,1)}, u32[]{:S(2)}, u32[]{:S(2)}) async-start(bf16[32,32,144]{2,1,0:T(8,128)(2,1)} %broadcast_in_dim.12), calls=%async_computation.1 | async-start | bytes 1048576 | tf_op jit(solution)/shard_map/all_to_all | solution.py:98
  109.5 15.8 %collective-permute-start.25 = (bf16[144,1024]{1,0:T(8,128)(2,1)S(1)}, bf16[144,1024]{1,0:T(8,128)(2,1)S(1)}, u32[]{:S(2)}, u32[]{:S(2)}) collective-permute-start(bf16[144,1024]{1,0:T(8,128)(2,1)S(1)} %get-tuple-element.38), channel_id=1, source_target_pairs={{0,14},{1,15},{2,0},{3,1},{4,2},{5,3},{6,4},{7,5},{8,6},{9,7},{10,... | collective-permute-start | bytes 884744 | tf_op jit(solution)/shard_map/ppermute | solution.py:85
  116.4 14.1 %collective-permute-start.19 = (bf16[144,1024]{1,0:T(8,128)(2,1)S(1)}, bf16[144,1024]{1,0:T(8,128)(2,1)S(1)}, u32[]{:S(2)}, u32[]{:S(2)}) collective-permute-start(bf16[144,1024]{1,0:T(8,128)(2,1)S(1)} %get-tuple-element.30), channel_id=1, source_target_pairs={{0,14},{1,15},{2,0},{3,1},{4,2},{5,3},{6,4},{7,5},{8,6},{9,7},{10,... | collective-permute-start | bytes 884744 | tf_op jit(solution)/shard_map/ppermute | solution.py:85
  119.9 14.2 %collective-permute-start.22 = (bf16[144,1024]{1,0:T(8,128)(2,1)S(1)}, bf16[144,1024]{1,0:T(8,128)(2,1)S(1)}, u32[]{:S(2)}, u32[]{:S(2)}) collective-permute-start(bf16[144,1024]{1,0:T(8,128)(2,1)S(1)} %get-tuple-element.34), channel_id=1, source_target_pairs={{0,2},{1,3},{2,4},{3,5},{4,6},{5,7},{6,8},{7,9},{8,10},{9,11},{10,... | collective-permute-start | bytes 884744 | tf_op jit(solution)/shard_map/ppermute | solution.py:85
  123.4 20.3 %collective-permute-start.16 = (bf16[144,1024]{1,0:T(8,128)(2,1)S(1)}, bf16[144,1024]{1,0:T(8,128)(2,1)S(1)}, u32[]{:S(2)}, u32[]{:S(2)}) collective-permute-start(bf16[144,1024]{1,0:T(8,128)(2,1)S(1)} %add_convert_fusion.10), channel_id=1, source_target_pairs={{0,2},{1,3},{2,4},{3,5},{4,6},{5,7},{6,8},{7,9},{8,10},{9,11},{10,... | collective-permute-start | bytes 884744 | tf_op jit(solution)/shard_map/ppermute | solution.py:85
  125.4 12.6 %collective-permute-start.26 = (bf16[144,1024]{1,0:T(8,128)(2,1)S(1)}, bf16[144,1024]{1,0:T(8,128)(2,1)S(1)}, u32[]{:S(2)}, u32[]{:S(2)}) collective-permute-start(bf16[144,1024]{1,0:T(8,128)(2,1)S(1)} %add_convert_fusion.3), channel_id=1, source_target_pairs={{0,14},{1,15},{2,0},{3,1},{4,2},{5,3},{6,4},{7,5},{8,6},{9,7},{10,... | collective-permute-start | bytes 884744 | tf_op jit(solution)/shard_map/ppermute | solution.py:85
  130.6 23.7 %collective-permute-start.20 = (bf16[144,1024]{1,0:T(8,128)(2,1)S(1)}, bf16[144,1024]{1,0:T(8,128)(2,1)S(1)}, u32[]{:S(2)}, u32[]{:S(2)}) collective-permute-start(bf16[144,1024]{1,0:T(8,128)(2,1)S(1)} %add_convert_fusion.7), channel_id=1, source_target_pairs={{0,14},{1,15},{2,0},{3,1},{4,2},{5,3},{6,4},{7,5},{8,6},{9,7},{10,... | collective-permute-start | bytes 884744 | tf_op jit(solution)/shard_map/ppermute | solution.py:85
  134.2 11.5 %collective-permute-start.23 = (bf16[144,1024]{1,0:T(8,128)(2,1)S(1)}, bf16[144,1024]{1,0:T(8,128)(2,1)S(1)}, u32[]{:S(2)}, u32[]{:S(2)}) collective-permute-start(bf16[144,1024]{1,0:T(8,128)(2,1)S(1)} %add_convert_fusion.5), channel_id=1, source_target_pairs={{0,2},{1,3},{2,4},{3,5},{4,6},{5,7},{6,8},{7,9},{8,10},{9,11},{10,... | collective-permute-start | bytes 884744 | tf_op jit(solution)/shard_map/ppermute | solution.py:85
  138.1 10.6 %collective-permute-start.27 = (bf16[144,1024]{1,0:T(8,128)(2,1)S(1)}, bf16[144,1024]{1,0:T(8,128)(2,1)S(1)}, u32[]{:S(2)}, u32[]{:S(2)}) collective-permute-start(bf16[144,1024]{1,0:T(8,128)(2,1)S(1)} %add_convert_fusion.2), channel_id=1, source_target_pairs={{0,14},{1,15},{2,0},{3,1},{4,2},{5,3},{6,4},{7,5},{8,6},{9,7},{10,... | collective-permute-start | bytes 884744 | tf_op jit(solution)/shard_map/ppermute | solution.py:85
  143.8 13.9 %collective-permute-start.17 = (bf16[144,1024]{1,0:T(8,128)(2,1)S(1)}, bf16[144,1024]{1,0:T(8,128)(2,1)S(1)}, u32[]{:S(2)}, u32[]{:S(2)}) collective-permute-start(bf16[144,1024]{1,0:T(8,128)(2,1)S(1)} %add_convert_fusion.9), channel_id=1, source_target_pairs={{0,2},{1,3},{2,4},{3,5},{4,6},{5,7},{6,8},{7,9},{8,10},{9,11},{10,... | collective-permute-start | bytes 884744 | tf_op jit(solution)/shard_map/ppermute | solution.py:85
  145.8 16.0 %collective-permute-start.24 = (bf16[144,1024]{1,0:T(8,128)(2,1)S(1)}, bf16[144,1024]{1,0:T(8,128)(2,1)S(1)}, u32[]{:S(2)}, u32[]{:S(2)}) collective-permute-start(bf16[144,1024]{1,0:T(8,128)(2,1)S(1)} %add_convert_fusion.4), channel_id=1, source_target_pairs={{0,2},{1,3},{2,4},{3,5},{4,6},{5,7},{6,8},{7,9},{8,10},{9,11},{10,... | collective-permute-start | bytes 884744 | tf_op jit(solution)/shard_map/ppermute | solution.py:85
  148.7 13.1 %collective-permute-start.28 = (bf16[144,1024]{1,0:T(8,128)(2,1)S(1)}, bf16[144,1024]{1,0:T(8,128)(2,1)S(1)}, u32[]{:S(2)}, u32[]{:S(2)}) collective-permute-start(bf16[144,1024]{1,0:T(8,128)(2,1)S(1)} %add_convert_fusion.1), channel_id=1, source_target_pairs={{0,14},{1,15},{2,0},{3,1},{4,2},{5,3},{6,4},{7,5},{8,6},{9,7},{10,... | collective-permute-start | bytes 884744 | tf_op jit(solution)/shard_map/ppermute | solution.py:85
  155.1 17.0 %collective-permute-start.21 = (bf16[144,1024]{1,0:T(8,128)(2,1)}, bf16[144,1024]{1,0:T(8,128)(2,1)S(1)}, u32[]{:S(2)}, u32[]{:S(2)}) collective-permute-start(bf16[144,1024]{1,0:T(8,128)(2,1)} %add_convert_fusion.6), channel_id=1, source_target_pairs={{0,14},{1,15},{2,0},{3,1},{4,2},{5,3},{6,4},{7,5},{8,6},{9,7},{10,... | collective-permute-start | bytes 884744 | tf_op jit(solution)/shard_map/ppermute | solution.py:85
  158.5 13.6 %collective-permute-start.18 = (bf16[144,1024]{1,0:T(8,128)(2,1)}, bf16[144,1024]{1,0:T(8,128)(2,1)S(1)}, u32[]{:S(2)}, u32[]{:S(2)}) collective-permute-start(bf16[144,1024]{1,0:T(8,128)(2,1)} %add_convert_fusion.8), channel_id=1, source_target_pairs={{0,2},{1,3},{2,4},{3,5},{4,6},{5,7},{6,8},{7,9},{8,10},{9,11},{10,... | collective-permute-start | bytes 884744 | tf_op jit(solution)/shard_map/ppermute | solution.py:85
  162.6 18.2 %collective-permute-start.29 = (bf16[144,1024]{1,0:T(8,128)(2,1)}, bf16[144,1024]{1,0:T(8,128)(2,1)}, u32[]{:S(2)}, u32[]{:S(2)}) collective-permute-start(bf16[144,1024]{1,0:T(8,128)(2,1)} %add_convert_fusion), channel_id=1, source_target_pairs={{0,1},{1,0},{2,3},{3,2},{4,5},{5,4},{6,7},{7,6},{8,9},{9,8},{10,11... | collective-permute-start | bytes 884744 | tf_op jit(solution)/shard_map/ppermute | solution.py:85
  (17 other events, 241.8 us)

commit v2 on v1

v2 whole, which is shorter than its diff:
```python
import functools

import jax
import jax.numpy as jnp
from jax import lax
from jax.experimental import pallas as pl
from jax.experimental.pallas import tpu as pltpu
from jax.sharding import PartitionSpec as P

HEAD_DIM = 128
ZS = 2
VMEM_LIMIT = 16 * 1024 * 1024
F32 = jnp.float32
BF16 = jnp.bfloat16


def after(value, *others):
    return lax.optimization_barrier((value, *others))[0]


def spec(space):
    return pl.BlockSpec(memory_space=space)


TURNED = (((0,), (0,)), ((), ()))


def product_body(first, ids, mine_ref, theirs_ref, *refs):
    chunks, (own_ref, partner_ref, w_ref) = refs[:-3], refs[-3:]
    rows, cols = chunks[0].shape[0], own_ref.shape[1]
    for n, chunk in enumerate(chunks):
        at = pl.multiple_of(ids[n] * rows, 16)
        w_ref[pl.ds(at, rows), :] = chunk[:, first : first + cols]
    partner_ref[...] = lax.dot_general(theirs_ref[...], w_ref[...], TURNED, preferred_element_type=F32).astype(BF16)
    own_ref[...] = lax.dot_general(mine_ref[...], w_ref[...], TURNED, preferred_element_type=F32)


def product(first, cols, ids, mine, theirs, chunks):
    tokens = mine.shape[1]
    return pl.pallas_call(
        functools.partial(product_body, first),
        out_shape=(jax.ShapeDtypeStruct((tokens, cols), F32), jax.ShapeDtypeStruct((tokens, cols), BF16)),
        in_specs=[spec(pltpu.SMEM)] + [spec(pltpu.VMEM)] * (2 + len(chunks)),
        out_specs=(spec(pltpu.VMEM),) * 2,
        scratch_shapes=[pltpu.VMEM((mine.shape[0], cols), BF16)],
        compiler_params=pltpu.CompilerParams(vmem_limit_bytes=VMEM_LIMIT),
        cost_estimate=pl.CostEstimate(flops=4 * mine.size * cols, bytes_accessed=4 << 20, transcendentals=0),
        name="product",
    )(ids, mine, theirs, *chunks)


def norm_body(first, own_ref, other_ref, cot_ref, keys_ref, slopes_ref):
    for head in range(0, own_ref.shape[1], HEAD_DIM):
        at = slice(head, head + HEAD_DIM)
        p = own_ref[:, at] + other_ref[:, at].astype(F32)
        inv = 1.0 / jnp.sqrt(jnp.mean(p * p, axis=-1, keepdims=True) + 1e-06)
        normed = p * inv
        g = cot_ref[:, first + head : first + head + HEAD_DIM].astype(F32)
        inner = jnp.mean(g * normed, axis=-1, keepdims=True)
        keys_ref[:, at] = normed.astype(BF16)
        slopes_ref[:, at] = ((g - normed * inner) * inv).astype(BF16)


def norm(first, own, other, cot):
    out = jax.ShapeDtypeStruct(own.shape, BF16)
    return pl.pallas_call(
        functools.partial(norm_body, first),
        out_shape=(out, out),
        in_specs=[spec(pltpu.VMEM)] * 3,
        out_specs=(spec(pltpu.VMEM),) * 2,
        compiler_params=pltpu.CompilerParams(vmem_limit_bytes=VMEM_LIMIT),
        cost_estimate=pl.CostEstimate(flops=own.size * 16, bytes_accessed=own.size * 12, transcendentals=0),
        name="norm",
    )(own, other, cot)


def partial_body(pieces, rows, ids, mine_ref, theirs_ref, *refs):
    slopes, outs = refs[: 2 * pieces], refs[2 * pieces :]
    cols = slopes[0].shape[1]
    for n, out in enumerate(outs):
        at = pl.multiple_of(ids[n] * rows, 16)
        for k in range(pieces):
            total = jnp.dot(mine_ref[pl.ds(at, rows), :], slopes[k][...], preferred_element_type=F32)
            total += jnp.dot(theirs_ref[pl.ds(at, rows), :], slopes[pieces + k][...], preferred_element_type=F32)
            out[:, k * cols : (k + 1) * cols] = total.astype(BF16)


def partials(rows, ids, mine, theirs, slopes, swapped):
    width = sum(s.shape[1] for s in slopes)
    out = jax.ShapeDtypeStruct((rows, width), BF16)
    return pl.pallas_call(
        functools.partial(partial_body, len(slopes), rows),
        out_shape=(out,) * len(ids),
        in_specs=[spec(pltpu.SMEM)] + [spec(pltpu.VMEM)] * (2 + 2 * len(slopes)),
        out_specs=(spec(pltpu.VMEM),) * len(ids),
        compiler_params=pltpu.CompilerParams(vmem_limit_bytes=VMEM_LIMIT),
        cost_estimate=pl.CostEstimate(
            flops=4 * len(ids) * rows * 256 * width, bytes_accessed=(2 << 20) + len(ids) * rows * 2048, transcendentals=0
        ),
        name="partials",
    )(jnp.stack(ids), mine, theirs, *slopes, *swapped)


def add_body(rows, plan, *refs):
    out_ref = refs[-1]
    for n, terms in enumerate(plan):
        blocks = [refs[i][row : row + rows, :] for i, row in terms]
        total = blocks[0]
        if len(blocks) > 1:
            total = sum(b.astype(F32) for b in blocks[1:]) + total.astype(F32)
        out_ref[n * rows : (n + 1) * rows, :] = total.astype(BF16)


def add(rows, plan, *inputs):
    height = rows * len(plan)
    return pl.pallas_call(
        functools.partial(add_body, rows, plan),
        out_shape=jax.ShapeDtypeStruct((height, inputs[0].shape[1]), BF16),
        in_specs=[spec(pltpu.VMEM)] * len(inputs),
        out_specs=spec(pltpu.VMEM),
        compiler_params=pltpu.CompilerParams(vmem_limit_bytes=8 * 1024 * 1024),
        cost_estimate=pl.CostEstimate(flops=height * 1024, bytes_accessed=height * 4096, transcendentals=0),
        name="add",
    )(*inputs)


def shards(inputs, cotangent, params, moment, second, drift, anchor, momentum):
    x, weights = inputs[0], params[0]
    rows = weights.shape[0]
    size = lax.axis_size("fsdp")
    ys = size // ZS
    index = lax.axis_index("fsdp").astype(jnp.int32)
    y, z = index // ZS, index % ZS
    half = ys // 2

    def step(value, dy, dz=0):
        pairs = [(i * ZS + j, ((i + dy) % ys) * ZS + (j + dz) % ZS) for i in range(ys) for j in range(ZS)]
        return lax.ppermute(value, "fsdp", pairs)

    def at(k):
        return (y + k) % ys

    own = weights.astype(BF16)
    blocks = x.T.reshape(ys, ZS, rows, x.shape[0])
    mine = lax.dynamic_index_in_dim(blocks, z, 1, False).reshape(ys * rows, x.shape[0])
    theirs = lax.dynamic_index_in_dim(blocks, 1 - z, 1, False).reshape(ys * rows, x.shape[0])
    leaving = theirs
    theirs = step(leaving, 0, 1)

    reps = lax.axis_size("rep")
    width = anchor.shape[1]
    sent = after(drift[0], leaving).T.reshape(reps, width, rows)
    drifts = lax.all_to_all(sent, "rep", split_axis=0, concat_axis=0, tiled=True)
    delta = jnp.sum(drifts.astype(F32), axis=0) / reps
    momentum_new = 0.9 * momentum.T + delta
    anchor_new = anchor.T - 0.7 * (delta + 0.9 * momentum_new)
    copies = jnp.broadcast_to(anchor_new.astype(BF16)[None], (reps, width, rows))

    ups, downs = [step(own, 1)], [step(own, -1)]
    for n in range(half - 2):
        ups.append(step(after(ups[-1], leaving) if n == 0 else ups[-1], 1))
        downs.append(step(after(downs[-1], leaving) if n == 0 else downs[-1], -1))
    ups.append(step(after(ups[-1], theirs), 1))
    chunks = [own] + ups + downs
    where = jnp.stack([at(0)] + [at(-1 - n) for n in range(half)] + [at(1 + n) for n in range(half - 1)])
    where, copies = lax.optimization_barrier((where, copies))

    cols = weights.shape[1] // 2
    own1, out1 = product(0, cols, where, mine, theirs, chunks)
    in1 = step(out1, 0, 1)
    own2, out2 = product(cols, cols, where, mine, theirs, chunks)
    in2 = step(out2, 0, 1)
    keys1, slopes1 = norm(0, own1, in1, cotangent[0])
    swapped1 = step(slopes1, 0, 1)
    keys2, slopes2 = norm(cols, own2, in2, cotangent[0])
    swapped2 = step(slopes2, 0, 1)
    keys = jnp.concatenate([keys1, keys2], axis=1)
    copies = after(copies, in1)
    anchors = lax.all_to_all(copies, "rep", split_axis=0, concat_axis=0, tiled=True)

    slopes, swapped = (slopes1, slopes2), (swapped1, swapped2)
    order = [half, 1 - half] + [s * k for k in range(half - 1, 0, -1) for s in (1, -1) if s * k != 1 - half] + [0]
    part = dict(zip(order[:2], partials(rows, [at(k) for k in order[:2]], mine, theirs, slopes, swapped)))
    part.update(zip(order[2:], partials(rows, [at(k) for k in order[2:]], mine, theirs, slopes, swapped)))
    two = [[(0, 0), (1, 0)]]
    au, ad = step(part[half], 1), step(part[1 - half], -1)
    rest = lax.optimization_barrier(0.3 * anchors.reshape(reps * width, rows).T.astype(F32))
    for k in range(half - 1, 0, -1):
        if k == half - 2:
            part[k] = after(part[k], rest)
        au = step(add(rows, two, part[k], au), 1)
        if k > 1:
            ad = step(add(rows, two, part[1 - k], ad), -1)
    gradient = part[0].astype(F32) + au.astype(F32) + ad.astype(F32)

    moment_one = 0.9 * moment[0] + 0.1 * gradient
    moment_two = 0.95 * second[0] + 0.05 * gradient * gradient
    stepped = weights - 0.4 * (moment_one / (jnp.sqrt(moment_two) + 1e-08) + 0.01 * weights)
    merged = rest + 0.7 * stepped
    return (merged[None], keys[None], anchor_new.T, momentum_new.T)


def solution(mesh):
    return jax.shard_map(
        shards,
        mesh=mesh,
        in_specs=(
            P("rep", "fsdp", None),
            P("rep", "fsdp", None),
            P("rep", "fsdp", None),
            P("rep", "fsdp", None),
            P("rep", "fsdp", None),
            P("rep", "fsdp", None),
            P("fsdp", "rep"),
            P("fsdp", "rep"),
        ),
        out_specs=(
            P("rep", "fsdp", None),
            P("rep", "fsdp", None),
            P("fsdp", "rep"),
            P("fsdp", "rep"),
        ),
        check_vma=False,
    )
```

time: 185 us -> 169 us (0.914)
  the two profiles are of different devices: /device:TPU:64 before, /device:TPU:2 now
where the time goes in v2:
time: 169 us; the launch traced here: 168 us
  starting transfers between devices  108 us (64%)
  waiting for transfers between devices  33.6 us (20%)
  local copies, waits for them, and re-layouts  8.68 us (5%)
  other arithmetic  8.19 us (5%)
  Pallas kernels  7.86 us (5%)
    ppermute x19, starting transfers between devices, step(): return lax.ppermute(value, 'fsdp', pairs)  76 us
    ppermute x19, waiting for transfers between devices, step(): return lax.ppermute(value, 'fsdp', pairs)  25.2 us
    all_to_all x1, starting transfers between devices, shards(): lax.all_to_all(copies, 'rep', split_axis=0, concat_axis=0, tiled=True)  24.2 us
    all_to_all x1, waiting for transfers between devices, shards(): lax.all_to_all(sent, 'rep', split_axis=0, concat_axis=0, tiled=True)  8.37 us
    all_to_all x1, starting transfers between devices, shards(): lax.all_to_all(sent, 'rep', split_axis=0, concat_axis=0, tiled=True)  7.77 us
    unnamed x36, local copies, waits for them, and re-layouts  5.23 us
  transfers between devices with their start and end apart: 21, of which 8 were waited for; matrix products, arithmetic and copies ran while one was open for 7% of the time, Pallas kernels for 4%

profile of v2, /device:TPU:2, one launch (start us, length us, event | category | flops | bytes accessed | tf_op | source)
XLA Modules:
  0.0 167.6 jit_solution(16935819123340388828)
XLA Ops:
  1.7 3.5 %collective-permute-start.1 = (bf16[144,1024]{1,0:T(8,128)(2,1)S(1)}, bf16[144,1024]{1,0:T(8,128)(2,1)S(1)}, u32[]{:S(2)}, u32[]{:S(2)}) collective-permute-start(bf16[144,1024]{1,0:T(8,128)(2,1)S(1)} %bitcast_convert_fusion.refs_0_), channel_id=1, source_target_pairs={{0,2},{1,3},{2,4},{3,5},{4,6},{5,7},{6,8},{7,9},{8,10},{9,11},{10,... | collective-permute-start | bytes 884744 | tf_op jit(solution)/shard_map/ppermute | solution.py:138
  5.2 3.8 %collective-permute-start.5 = (bf16[144,1024]{1,0:T(8,128)(2,1)S(1)}, bf16[144,1024]{1,0:T(8,128)(2,1)S(1)}, u32[]{:S(2)}, u32[]{:S(2)}) collective-permute-start(bf16[144,1024]{1,0:T(8,128)(2,1)S(1)} %bitcast_convert_fusion.refs_0_), channel_id=1, source_target_pairs={{0,14},{1,15},{2,0},{3,1},{4,2},{5,3},{6,4},{7,5},{8,6},{9,7},{10,... | collective-permute-start | bytes 884744 | tf_op jit(solution)/shard_map/ppermute | solution.py:138
  9.1 1.6 copy.16
  11.6 10.9 %collective-permute-start = (bf16[1152,256]{1,0:T(8,128)(2,1)}, bf16[1152,256]{1,0:T(8,128)(2,1)S(1)}, u32[]{:S(2)}, u32[]{:S(2)}) collective-permute-start(bf16[1152,256]{1,0:T(8,128)(2,1)} %bitcast.13), channel_id=1, source_target_pairs={{0,1},{1,0},{2,3},{3,2},{4,5},{5,4},{6,7},{7,6},{8,9},{9,8},{10,11... | collective-permute-start | bytes 1769480 | tf_op jit(solution)/shard_map/ppermute | solution.py:138
  22.5 2.0 %collective-permute-start.2 = (bf16[144,1024]{1,0:T(8,128)(2,1)S(1)}, bf16[144,1024]{1,0:T(8,128)(2,1)S(1)}, u32[]{:S(2)}, u32[]{:S(2)}) collective-permute-start(bf16[144,1024]{1,0:T(8,128)(2,1)S(1)} %collective-permute-done.1.refs_1_), channel_id=1, source_target_pairs={{0,2},{1,3},{2,4},{3,5},{4,6},{5,7},{6,8},{7,9},{8,10},{9,11},{10,... | collective-permute-start | bytes 884744 | tf_op jit(solution)/shard_map/ppermute | solution.py:138
  25.5 7.8 %all-to-all-start = ((bf16[32,32,144]{2,1,0:T(8,128)(2,1)}), bf16[32,32,144]{2,1,0:T(8,128)(2,1)}, u32[]{:S(2)}, u32[]{:S(2)}) async-start(bf16[32,32,144]{2,1,0:T(8,128)(2,1)} %bitcast.15), calls=%async_computation | async-start | bytes 1048576 | tf_op jit(solution)/shard_map/all_to_all | solution.py:153
  33.3 5.0 %collective-permute-start.6 = (bf16[144,1024]{1,0:T(8,128)(2,1)S(1)}, bf16[144,1024]{1,0:T(8,128)(2,1)S(1)}, u32[]{:S(2)}, u32[]{:S(2)}) collective-permute-start(bf16[144,1024]{1,0:T(8,128)(2,1)S(1)} %collective-permute-done.5.refs_5_), channel_id=1, source_target_pairs={{0,14},{1,15},{2,0},{3,1},{4,2},{5,3},{6,4},{7,5},{8,6},{9,7},{10,... | collective-permute-start | bytes 884744 | tf_op jit(solution)/shard_map/ppermute | solution.py:138
  38.4 1.9 %collective-permute-start.3 = (bf16[144,1024]{1,0:T(8,128)(2,1)S(1)}, bf16[144,1024]{1,0:T(8,128)(2,1)S(1)}, u32[]{:S(2)}, u32[]{:S(2)}) collective-permute-start(bf16[144,1024]{1,0:T(8,128)(2,1)S(1)} %collective-permute-done.2.refs_2_), channel_id=1, source_target_pairs={{0,2},{1,3},{2,4},{3,5},{4,6},{5,7},{6,8},{7,9},{8,10},{9,11},{10,... | collective-permute-start | bytes 884744 | tf_op jit(solution)/shard_map/ppermute | solution.py:138
  40.5 4.4 %collective-permute-done.6.refs_6_ = bf16[144,1024]{1,0:T(8,128)(2,1)S(1)} collective-permute-done((bf16[144,1024]{1,0:T(8,128)(2,1)S(1)}, bf16[144,1024]{1,0:T(8,128)(2,1)S(1)}, u32[]{:S(2)}, u32[]{:S(2)}) %collective-permute-start.6) | collective-permute-done | bytes 294944 | tf_op jit(solution)/shard_map/ppermute | solution.py:138
  44.9 5.6 %collective-permute-start.7 = (bf16[144,1024]{1,0:T(8,128)(2,1)S(1)}, bf16[144,1024]{1,0:T(8,128)(2,1)S(1)}, u32[]{:S(2)}, u32[]{:S(2)}) collective-permute-start(bf16[144,1024]{1,0:T(8,128)(2,1)S(1)} %collective-permute-done.6.refs_6_), channel_id=1, source_target_pairs={{0,14},{1,15},{2,0},{3,1},{4,2},{5,3},{6,4},{7,5},{8,6},{9,7},{10,... | collective-permute-start | bytes 884744 | tf_op jit(solution)/shard_map/ppermute | solution.py:138
  50.5 1.9 %collective-permute-start.4 = (bf16[144,1024]{1,0:T(8,128)(2,1)S(1)}, bf16[144,1024]{1,0:T(8,128)(2,1)S(1)}, u32[]{:S(2)}, u32[]{:S(2)}) collective-permute-start(bf16[144,1024]{1,0:T(8,128)(2,1)S(1)} %collective-permute-done.3.refs_3_), channel_id=1, source_target_pairs={{0,2},{1,3},{2,4},{3,5},{4,6},{5,7},{6,8},{7,9},{8,10},{9,11},{10,... | collective-permute-start | bytes 884744 | tf_op jit(solution)/shard_map/ppermute | solution.py:138
  52.5 8.4 %all-to-all-done = bf16[32,32,144]{2,1,0:T(8,128)(2,1)} async-done(((bf16[32,32,144]{2,1,0:T(8,128)(2,1)}), bf16[32,32,144]{2,1,0:T(8,128)(2,1)}, u32[]{:S(2)}, u32[]{:S(2)}) %all-to-all-start) | async-done | bytes 294944 | tf_op jit(solution)/shard_map/all_to_all | solution.py:153
  65.1 4.2 %collective-permute-start.9 = (bf16[256,512]{1,0:T(8,128)(2,1)S(1)}, bf16[256,512]{1,0:T(8,128)(2,1)S(1)}, u32[]{:S(2)}, u32[]{:S(2)}) collective-permute-start(bf16[256,512]{1,0:T(8,128)(2,1)S(1)} %get-tuple-element.39), channel_id=1, source_target_pairs={{0,1},{1,0},{2,3},{3,2},{4,5},{5,4},{6,7},{7,6},{8,9},{9,8},{10,11... | collective-permute-start | bytes 786440 | tf_op jit(solution)/shard_map/ppermute | solution.py:138
  70.9 5.6 %collective-permute-start.8 = (bf16[256,512]{1,0:T(8,128)(2,1)S(1)}, bf16[256,512]{1,0:T(8,128)(2,1)S(1)}, u32[]{:S(2)}, u32[]{:S(2)}) collective-permute-start(bf16[256,512]{1,0:T(8,128)(2,1)S(1)} %get-tuple-element.34), channel_id=1, source_target_pairs={{0,1},{1,0},{2,3},{3,2},{4,5},{5,4},{6,7},{7,6},{8,9},{9,8},{10,11... | collective-permute-start | bytes 786440 | tf_op jit(solution)/shard_map/ppermute | solution.py:138
  76.5 5.2 %collective-permute-done.9.other_ref = bf16[256,512]{1,0:T(8,128)(2,1)S(1)} collective-permute-done((bf16[256,512]{1,0:T(8,128)(2,1)S(1)}, bf16[256,512]{1,0:T(8,128)(2,1)S(1)}, u32[]{:S(2)}, u32[]{:S(2)}) %collective-permute-start.9) | collective-permute-done | bytes 262176 | tf_op jit(solution)/shard_map/ppermute | solution.py:138
  82.3 4.0 %collective-permute-start.11 = (bf16[256,512]{1,0:T(8,128)(2,1)S(1)}, bf16[256,512]{1,0:T(8,128)(2,1)S(1)}, u32[]{:S(2)}, u32[]{:S(2)}) collective-permute-start(bf16[256,512]{1,0:T(8,128)(2,1)S(1)} %get-tuple-element.40.refs_1_), channel_id=1, source_target_pairs={{0,1},{1,0},{2,3},{3,2},{4,5},{5,4},{6,7},{7,6},{8,9},{9,8},{10,11... | collective-permute-start | bytes 786440 | tf_op jit(solution)/shard_map/ppermute | solution.py:138
  86.3 4.1 %collective-permute-done.8.other_ref = bf16[256,512]{1,0:T(8,128)(2,1)S(1)} collective-permute-done((bf16[256,512]{1,0:T(8,128)(2,1)S(1)}, bf16[256,512]{1,0:T(8,128)(2,1)S(1)}, u32[]{:S(2)}, u32[]{:S(2)}) %collective-permute-start.8) | collective-permute-done | bytes 262176 | tf_op jit(solution)/shard_map/ppermute | solution.py:138
  91.7 4.2 %collective-permute-start.10 = (bf16[256,512]{1,0:T(8,128)(2,1)S(1)}, bf16[256,512]{1,0:T(8,128)(2,1)S(1)}, u32[]{:S(2)}, u32[]{:S(2)}) collective-permute-start(bf16[256,512]{1,0:T(8,128)(2,1)S(1)} %get-tuple-element.37.refs_0_), channel_id=1, source_target_pairs={{0,1},{1,0},{2,3},{3,2},{4,5},{5,4},{6,7},{7,6},{8,9},{9,8},{10,11... | collective-permute-start | bytes 786440 | tf_op jit(solution)/shard_map/ppermute | solution.py:138
  95.8 24.2 %all-to-all-start.1 = ((bf16[32,32,144]{2,1,0:T(8,128)(2,1)}), bf16[32,32,144]{2,1,0:T(8,128)(2,1)}, u32[]{:S(2)}, u32[]{:S(2)}) async-start(bf16[32,32,144]{2,1,0:T(8,128)(2,1)} %broadcast_in_dim.12), calls=%async_computation.1 | async-start | bytes 1048576 | tf_op jit(solution)/shard_map/all_to_all | solution.py:179
  120.2 1.7 %partials.3 = (bf16[144,1024]{1,0:T(8,128)(2,1)}, bf16[144,1024]{1,0:T(8,128)(2,1)}) custom-call(s32[2]{0:T(128)S(1)} %pad_add_fusion.ids, bf16[1152,256]{1,0:T(8,128)(2,1)S(1)} %bitcast.69, bf16[1152,256]{1,0:T(8,128)(2,1)S(1)} %collective-permute-done.theirs_ref, bf16[256,512]{1,0:T(8,128)(2,1)S(1)} %get-tuple-element.37.refs_0_, ...), custom_call_target="tpu_custom_call" | custom-call | flops 301989888 | bytes 2686976 | tf_op jit(solution)/shard_map/partials/pallas_call | solution.py:91
  121.9 1.9 %collective-permute-start.12 = (bf16[144,1024]{1,0:T(8,128)(2,1)}, bf16[144,1024]{1,0:T(8,128)(2,1)S(1)}, u32[]{:S(2)}, u32[]{:S(2)}) collective-permute-start(bf16[144,1024]{1,0:T(8,128)(2,1)} %get-tuple-element.46), channel_id=1, source_target_pairs={{0,2},{1,3},{2,4},{3,5},{4,6},{5,7},{6,8},{7,9},{8,10},{9,11},{10,... | collective-permute-start | bytes 884744 | tf_op jit(solution)/shard_map/ppermute | solution.py:138
  123.8 5.1 %collective-permute-start.16 = (bf16[144,1024]{1,0:T(8,128)(2,1)}, bf16[144,1024]{1,0:T(8,128)(2,1)S(1)}, u32[]{:S(2)}, u32[]{:S(2)}) collective-permute-start(bf16[144,1024]{1,0:T(8,128)(2,1)} %get-tuple-element.49), channel_id=1, source_target_pairs={{0,14},{1,15},{2,0},{3,1},{4,2},{5,3},{6,4},{7,5},{8,6},{9,7},{10,... | collective-permute-start | bytes 884744 | tf_op jit(solution)/shard_map/ppermute | solution.py:138
  131.0 1.6 partials.2
  132.6 1.7 collective-permute-done.12.refs_1_
  134.4 1.9 %collective-permute-start.13 = (bf16[144,1024]{1,0:T(8,128)(2,1)S(1)}, bf16[144,1024]{1,0:T(8,128)(2,1)S(1)}, u32[]{:S(2)}, u32[]{:S(2)}) collective-permute-start(bf16[144,1024]{1,0:T(8,128)(2,1)S(1)} %add.220), channel_id=1, source_target_pairs={{0,2},{1,3},{2,4},{3,5},{4,6},{5,7},{6,8},{7,9},{8,10},{9,11},{10,... | collective-permute-start | bytes 884744 | tf_op jit(solution)/shard_map/ppermute | solution.py:138
  136.4 5.1 %collective-permute-start.17 = (bf16[144,1024]{1,0:T(8,128)(2,1)S(1)}, bf16[144,1024]{1,0:T(8,128)(2,1)S(1)}, u32[]{:S(2)}, u32[]{:S(2)}) collective-permute-start(bf16[144,1024]{1,0:T(8,128)(2,1)S(1)} %add.223), channel_id=1, source_target_pairs={{0,14},{1,15},{2,0},{3,1},{4,2},{5,3},{6,4},{7,5},{8,6},{9,7},{10,... | collective-permute-start | bytes 884744 | tf_op jit(solution)/shard_map/ppermute | solution.py:138
  141.5 2.2 %convert_multiply_fusion = f32[32,32,144]{2,1,0:T(8,128)} fusion(bf16[32,32,144]{2,1,0:T(8,128)(2,1)} %all-to-all-done.1), kind=kLoop, calls=%fused_computation | loop fusion | flops 294912 | bytes 884736 | tf_op jit(solution)/shard_map/mul | solution.py:187
  145.8 2.1 %collective-permute-start.14 = (bf16[144,1024]{1,0:T(8,128)(2,1)S(1)}, bf16[144,1024]{1,0:T(8,128)(2,1)S(1)}, u32[]{:S(2)}, u32[]{:S(2)}) collective-permute-start(bf16[144,1024]{1,0:T(8,128)(2,1)S(1)} %add.221), channel_id=1, source_target_pairs={{0,2},{1,3},{2,4},{3,5},{4,6},{5,7},{6,8},{7,9},{8,10},{9,11},{10,... | collective-permute-start | bytes 884744 | tf_op jit(solution)/shard_map/ppermute | solution.py:138
  148.0 5.3 %collective-permute-start.18 = (bf16[144,1024]{1,0:T(8,128)(2,1)S(1)}, bf16[144,1024]{1,0:T(8,128)(2,1)S(1)}, u32[]{:S(2)}, u32[]{:S(2)}) collective-permute-start(bf16[144,1024]{1,0:T(8,128)(2,1)S(1)} %add.224), channel_id=1, source_target_pairs={{0,14},{1,15},{2,0},{3,1},{4,2},{5,3},{6,4},{7,5},{8,6},{9,7},{10,... | collective-permute-start | bytes 884744 | tf_op jit(solution)/shard_map/ppermute | solution.py:138
  153.3 3.1 %collective-permute-done.14.refs_1_ = bf16[144,1024]{1,0:T(8,128)(2,1)S(1)} collective-permute-done((bf16[144,1024]{1,0:T(8,128)(2,1)S(1)}, bf16[144,1024]{1,0:T(8,128)(2,1)S(1)}, u32[]{:S(2)}, u32[]{:S(2)}) %collective-permute-start.14) | collective-permute-done | bytes 294944 | tf_op jit(solution)/shard_map/ppermute | solution.py:138
  156.4 1.9 %collective-permute-start.15 = (bf16[144,1024]{1,0:T(8,128)(2,1)S(1)}, bf16[144,1024]{1,0:T(8,128)(2,1)S(1)}, u32[]{:S(2)}, u32[]{:S(2)}) collective-permute-start(bf16[144,1024]{1,0:T(8,128)(2,1)S(1)} %add.222), channel_id=1, source_target_pairs={{0,2},{1,3},{2,4},{3,5},{4,6},{5,7},{6,8},{7,9},{8,10},{9,11},{10,... | collective-permute-start | bytes 884744 | tf_op jit(solution)/shard_map/ppermute | solution.py:138
  159.9 6.4 %collective-permute-done.15 = bf16[144,1024]{1,0:T(8,128)(2,1)S(1)} collective-permute-done((bf16[144,1024]{1,0:T(8,128)(2,1)S(1)}, bf16[144,1024]{1,0:T(8,128)(2,1)S(1)}, u32[]{:S(2)}, u32[]{:S(2)}) %collective-permute-start.15) | collective-permute-done | bytes 294944 | tf_op jit(solution)/shard_map/ppermute | solution.py:138
  (70 shorter events, 18.1 us)
Async XLA Ops:
  1.7 20.7 %collective-permute-start.1 = (bf16[144,1024]{1,0:T(8,128)(2,1)S(1)}, bf16[144,1024]{1,0:T(8,128)(2,1)S(1)}, u32[]{:S(2)}, u32[]{:S(2)}) collective-permute-start(bf16[144,1024]{1,0:T(8,128)(2,1)S(1)} %bitcast_convert_fusion.refs_0_), channel_id=1, source_target_pairs={{0,2},{1,3},{2,4},{3,5},{4,6},{5,7},{6,8},{7,9},{8,10},{9,11},{10,... | collective-permute-start | bytes 884744 | tf_op jit(solution)/shard_map/ppermute | solution.py:138
  5.2 28.1 %collective-permute-start.5 = (bf16[144,1024]{1,0:T(8,128)(2,1)S(1)}, bf16[144,1024]{1,0:T(8,128)(2,1)S(1)}, u32[]{:S(2)}, u32[]{:S(2)}) collective-permute-start(bf16[144,1024]{1,0:T(8,128)(2,1)S(1)} %bitcast_convert_fusion.refs_0_), channel_id=1, source_target_pairs={{0,14},{1,15},{2,0},{3,1},{4,2},{5,3},{6,4},{7,5},{8,6},{9,7},{10,... | collective-permute-start | bytes 884744 | tf_op jit(solution)/shard_map/ppermute | solution.py:138
  10.7 13.9 %copy-start.12 = (bf16[1,144,1024]{2,1,0:T(8,128)(2,1)S(1)}, bf16[1,144,1024]{2,1,0:T(8,128)(2,1)}, u32[]{:S(2)}) copy-start(bf16[1,144,1024]{2,1,0:T(8,128)(2,1)} %param.13) | copy-start | bytes 884740
  11.6 39.0 %collective-permute-start = (bf16[1152,256]{1,0:T(8,128)(2,1)}, bf16[1152,256]{1,0:T(8,128)(2,1)S(1)}, u32[]{:S(2)}, u32[]{:S(2)}) collective-permute-start(bf16[1152,256]{1,0:T(8,128)(2,1)} %bitcast.13), channel_id=1, source_target_pairs={{0,1},{1,0},{2,3},{3,2},{4,5},{5,4},{6,7},{7,6},{8,9},{9,8},{10,11... | collective-permute-start | bytes 1769480 | tf_op jit(solution)/shard_map/ppermute | solution.py:138
  22.5 15.9 %collective-permute-start.2 = (bf16[144,1024]{1,0:T(8,128)(2,1)S(1)}, bf16[144,1024]{1,0:T(8,128)(2,1)S(1)}, u32[]{:S(2)}, u32[]{:S(2)}) collective-permute-start(bf16[144,1024]{1,0:T(8,128)(2,1)S(1)} %collective-permute-done.1.refs_1_), channel_id=1, source_target_pairs={{0,2},{1,3},{2,4},{3,5},{4,6},{5,7},{6,8},{7,9},{8,10},{9,11},{10,... | collective-permute-start | bytes 884744 | tf_op jit(solution)/shard_map/ppermute | solution.py:138
  25.5 35.3 %all-to-all-start = ((bf16[32,32,144]{2,1,0:T(8,128)(2,1)}), bf16[32,32,144]{2,1,0:T(8,128)(2,1)}, u32[]{:S(2)}, u32[]{:S(2)}) async-start(bf16[32,32,144]{2,1,0:T(8,128)(2,1)} %bitcast.15), calls=%async_computation | async-start | bytes 1048576 | tf_op jit(solution)/shard_map/all_to_all | solution.py:153
  33.3 11.6 %collective-permute-start.6 = (bf16[144,1024]{1,0:T(8,128)(2,1)S(1)}, bf16[144,1024]{1,0:T(8,128)(2,1)S(1)}, u32[]{:S(2)}, u32[]{:S(2)}) collective-permute-start(bf16[144,1024]{1,0:T(8,128)(2,1)S(1)} %collective-permute-done.5.refs_5_), channel_id=1, source_target_pairs={{0,14},{1,15},{2,0},{3,1},{4,2},{5,3},{6,4},{7,5},{8,6},{9,7},{10,... | collective-permute-start | bytes 884744 | tf_op jit(solution)/shard_map/ppermute | solution.py:138
  38.4 12.2 %collective-permute-start.3 = (bf16[144,1024]{1,0:T(8,128)(2,1)S(1)}, bf16[144,1024]{1,0:T(8,128)(2,1)S(1)}, u32[]{:S(2)}, u32[]{:S(2)}) collective-permute-start(bf16[144,1024]{1,0:T(8,128)(2,1)S(1)} %collective-permute-done.2.refs_2_), channel_id=1, source_target_pairs={{0,2},{1,3},{2,4},{3,5},{4,6},{5,7},{6,8},{7,9},{8,10},{9,11},{10,... | collective-permute-start | bytes 884744 | tf_op jit(solution)/shard_map/ppermute | solution.py:138
  44.9 18.7 %collective-permute-start.7 = (bf16[144,1024]{1,0:T(8,128)(2,1)S(1)}, bf16[144,1024]{1,0:T(8,128)(2,1)S(1)}, u32[]{:S(2)}, u32[]{:S(2)}) collective-permute-start(bf16[144,1024]{1,0:T(8,128)(2,1)S(1)} %collective-permute-done.6.refs_6_), channel_id=1, source_target_pairs={{0,14},{1,15},{2,0},{3,1},{4,2},{5,3},{6,4},{7,5},{8,6},{9,7},{10,... | collective-permute-start | bytes 884744 | tf_op jit(solution)/shard_map/ppermute | solution.py:138
  50.5 13.1 %collective-permute-start.4 = (bf16[144,1024]{1,0:T(8,128)(2,1)S(1)}, bf16[144,1024]{1,0:T(8,128)(2,1)S(1)}, u32[]{:S(2)}, u32[]{:S(2)}) collective-permute-start(bf16[144,1024]{1,0:T(8,128)(2,1)S(1)} %collective-permute-done.3.refs_3_), channel_id=1, source_target_pairs={{0,2},{1,3},{2,4},{3,5},{4,6},{5,7},{6,8},{7,9},{8,10},{9,11},{10,... | collective-permute-start | bytes 884744 | tf_op jit(solution)/shard_map/ppermute | solution.py:138
  65.1 16.6 %copy-start = (bf16[1,256,1024]{2,1,0:T(8,128)(2,1)S(1)}, bf16[1,256,1024]{2,1,0:T(8,128)(2,1)}, u32[]{:S(2)}) copy-start(bf16[1,256,1024]{2,1,0:T(8,128)(2,1)} %param.9) | copy-start | bytes 1572868
  65.1 16.5 %collective-permute-start.9 = (bf16[256,512]{1,0:T(8,128)(2,1)S(1)}, bf16[256,512]{1,0:T(8,128)(2,1)S(1)}, u32[]{:S(2)}, u32[]{:S(2)}) collective-permute-start(bf16[256,512]{1,0:T(8,128)(2,1)S(1)} %get-tuple-element.39), channel_id=1, source_target_pairs={{0,1},{1,0},{2,3},{3,2},{4,5},{5,4},{6,7},{7,6},{8,9},{9,8},{10,11... | collective-permute-start | bytes 786440 | tf_op jit(solution)/shard_map/ppermute | solution.py:138
  70.9 19.5 %collective-permute-start.8 = (bf16[256,512]{1,0:T(8,128)(2,1)S(1)}, bf16[256,512]{1,0:T(8,128)(2,1)S(1)}, u32[]{:S(2)}, u32[]{:S(2)}) collective-permute-start(bf16[256,512]{1,0:T(8,128)(2,1)S(1)} %get-tuple-element.34), channel_id=1, source_target_pairs={{0,1},{1,0},{2,3},{3,2},{4,5},{5,4},{6,7},{7,6},{8,9},{9,8},{10,11... | collective-permute-start | bytes 786440 | tf_op jit(solution)/shard_map/ppermute | solution.py:138
  82.3 37.9 %collective-permute-start.11 = (bf16[256,512]{1,0:T(8,128)(2,1)S(1)}, bf16[256,512]{1,0:T(8,128)(2,1)S(1)}, u32[]{:S(2)}, u32[]{:S(2)}) collective-permute-start(bf16[256,512]{1,0:T(8,128)(2,1)S(1)} %get-tuple-element.40.refs_1_), channel_id=1, source_target_pairs={{0,1},{1,0},{2,3},{3,2},{4,5},{5,4},{6,7},{7,6},{8,9},{9,8},{10,11... | collective-permute-start | bytes 786440 | tf_op jit(solution)/shard_map/ppermute | solution.py:138
  91.7 30.3 %copy-start.1 = (bf16[256,512]{1,0:T(8,128)(2,1)}, bf16[256,512]{1,0:T(8,128)(2,1)S(1)}, u32[]{:S(2)}) copy-start(bf16[256,512]{1,0:T(8,128)(2,1)S(1)} %get-tuple-element.37.refs_0_) | copy-start | bytes 786436
  91.7 28.5 %collective-permute-start.10 = (bf16[256,512]{1,0:T(8,128)(2,1)S(1)}, bf16[256,512]{1,0:T(8,128)(2,1)S(1)}, u32[]{:S(2)}, u32[]{:S(2)}) collective-permute-start(bf16[256,512]{1,0:T(8,128)(2,1)S(1)} %get-tuple-element.37.refs_0_), channel_id=1, source_target_pairs={{0,1},{1,0},{2,3},{3,2},{4,5},{5,4},{6,7},{7,6},{8,9},{9,8},{10,11... | collective-permute-start | bytes 786440 | tf_op jit(solution)/shard_map/ppermute | solution.py:138
  95.8 45.7 %all-to-all-start.1 = ((bf16[32,32,144]{2,1,0:T(8,128)(2,1)}), bf16[32,32,144]{2,1,0:T(8,128)(2,1)}, u32[]{:S(2)}, u32[]{:S(2)}) async-start(bf16[32,32,144]{2,1,0:T(8,128)(2,1)} %broadcast_in_dim.12), calls=%async_computation.1 | async-start | bytes 1048576 | tf_op jit(solution)/shard_map/all_to_all | solution.py:179
  121.9 12.4 %collective-permute-start.12 = (bf16[144,1024]{1,0:T(8,128)(2,1)}, bf16[144,1024]{1,0:T(8,128)(2,1)S(1)}, u32[]{:S(2)}, u32[]{:S(2)}) collective-permute-start(bf16[144,1024]{1,0:T(8,128)(2,1)} %get-tuple-element.46), channel_id=1, source_target_pairs={{0,2},{1,3},{2,4},{3,5},{4,6},{5,7},{6,8},{7,9},{8,10},{9,11},{10,... | collective-permute-start | bytes 884744 | tf_op jit(solution)/shard_map/ppermute | solution.py:138
  123.8 12.5 %collective-permute-start.16 = (bf16[144,1024]{1,0:T(8,128)(2,1)}, bf16[144,1024]{1,0:T(8,128)(2,1)S(1)}, u32[]{:S(2)}, u32[]{:S(2)}) collective-permute-start(bf16[144,1024]{1,0:T(8,128)(2,1)} %get-tuple-element.49), channel_id=1, source_target_pairs={{0,14},{1,15},{2,0},{3,1},{4,2},{5,3},{6,4},{7,5},{8,6},{9,7},{10,... | collective-permute-start | bytes 884744 | tf_op jit(solution)/shard_map/ppermute | solution.py:138
  134.4 11.3 %collective-permute-start.13 = (bf16[144,1024]{1,0:T(8,128)(2,1)S(1)}, bf16[144,1024]{1,0:T(8,128)(2,1)S(1)}, u32[]{:S(2)}, u32[]{:S(2)}) collective-permute-start(bf16[144,1024]{1,0:T(8,128)(2,1)S(1)} %add.220), channel_id=1, source_target_pairs={{0,2},{1,3},{2,4},{3,5},{4,6},{5,7},{6,8},{7,9},{8,10},{9,11},{10,... | collective-permute-start | bytes 884744 | tf_op jit(solution)/shard_map/ppermute | solution.py:138
  136.4 11.5 %collective-permute-start.17 = (bf16[144,1024]{1,0:T(8,128)(2,1)S(1)}, bf16[144,1024]{1,0:T(8,128)(2,1)S(1)}, u32[]{:S(2)}, u32[]{:S(2)}) collective-permute-start(bf16[144,1024]{1,0:T(8,128)(2,1)S(1)} %add.223), channel_id=1, source_target_pairs={{0,14},{1,15},{2,0},{3,1},{4,2},{5,3},{6,4},{7,5},{8,6},{9,7},{10,... | collective-permute-start | bytes 884744 | tf_op jit(solution)/shard_map/ppermute | solution.py:138
  145.2 13.1 %copy-start.14 = (f32[32,144]{1,0:T(8,128)S(1)}, f32[32,144]{1,0:T(8,128)}, u32[]{:S(2)}) copy-start(f32[32,144]{1,0:T(8,128)} %copy-done.13) | copy-start | bytes 55300
  145.2 13.1 %copy-start.15 = (f32[144,32]{0,1:T(8,128)S(1)}, f32[144,32]{0,1:T(8,128)}, u32[]{:S(2)}) copy-start(f32[144,32]{0,1:T(8,128)} %param.14) | copy-start | bytes 55300
  145.2 13.1 %copy-start.16 = (f32[144,32]{0,1:T(8,128)S(1)}, f32[144,32]{0,1:T(8,128)}, u32[]{:S(2)}) copy-start(f32[144,32]{0,1:T(8,128)} %param.15) | copy-start | bytes 55300
  145.8 13.2 %copy-start.6 = (bf16[256,512]{1,0:T(8,128)(2,1)S(1)}, bf16[256,512]{1,0:T(8,128)(2,1)}, u32[]{:S(2)}) copy-start(bf16[256,512]{1,0:T(8,128)(2,1)} %copy-done.5) | copy-start | bytes 786436
  145.8 13.2 %copy-start.8 = (bf16[256,512]{1,0:T(8,128)(2,1)S(1)}, bf16[256,512]{1,0:T(8,128)(2,1)}, u32[]{:S(2)}) copy-start(bf16[256,512]{1,0:T(8,128)(2,1)} %copy-done.7) | copy-start | bytes 786436
  145.8 10.5 %collective-permute-start.14 = (bf16[144,1024]{1,0:T(8,128)(2,1)S(1)}, bf16[144,1024]{1,0:T(8,128)(2,1)S(1)}, u32[]{:S(2)}, u32[]{:S(2)}) collective-permute-start(bf16[144,1024]{1,0:T(8,128)(2,1)S(1)} %add.221), channel_id=1, source_target_pairs={{0,2},{1,3},{2,4},{3,5},{4,6},{5,7},{6,8},{7,9},{8,10},{9,11},{10,... | collective-permute-start | bytes 884744 | tf_op jit(solution)/shard_map/ppermute | solution.py:138
  147.9 18.3 %copy-start.9 = (f32[1,144,1024]{2,1,0:T(8,128)S(1)}, f32[1,144,1024]{2,1,0:T(8,128)}, u32[]{:S(2)}) copy-start(f32[1,144,1024]{2,1,0:T(8,128)} %param.10) | copy-start | bytes 1769476
  148.0 18.3 %copy-start.10 = (f32[1,144,1024]{2,1,0:T(8,128)S(1)}, f32[1,144,1024]{2,1,0:T(8,128)}, u32[]{:S(2)}) copy-start(f32[1,144,1024]{2,1,0:T(8,128)} %param.12) | copy-start | bytes 1769476
  148.0 18.3 %copy-start.11 = (f32[1,144,1024]{2,1,0:T(8,128)S(1)}, f32[1,144,1024]{2,1,0:T(8,128)}, u32[]{:S(2)}) copy-start(f32[1,144,1024]{2,1,0:T(8,128)} %param.11) | copy-start | bytes 1769476
  148.0 11.9 %collective-permute-start.18 = (bf16[144,1024]{1,0:T(8,128)(2,1)S(1)}, bf16[144,1024]{1,0:T(8,128)(2,1)S(1)}, u32[]{:S(2)}, u32[]{:S(2)}) collective-permute-start(bf16[144,1024]{1,0:T(8,128)(2,1)S(1)} %add.224), channel_id=1, source_target_pairs={{0,14},{1,15},{2,0},{3,1},{4,2},{5,3},{6,4},{7,5},{8,6},{9,7},{10,... | collective-permute-start | bytes 884744 | tf_op jit(solution)/shard_map/ppermute | solution.py:138
  156.4 9.8 %collective-permute-start.15 = (bf16[144,1024]{1,0:T(8,128)(2,1)S(1)}, bf16[144,1024]{1,0:T(8,128)(2,1)S(1)}, u32[]{:S(2)}, u32[]{:S(2)}) collective-permute-start(bf16[144,1024]{1,0:T(8,128)(2,1)S(1)} %add.222), channel_id=1, source_target_pairs={{0,2},{1,3},{2,4},{3,5},{4,6},{5,7},{6,8},{7,9},{8,10},{9,11},{10,... | collective-permute-start | bytes 884744 | tf_op jit(solution)/shard_map/ppermute | solution.py:138
  (6 other events, 21.7 us)

commit v3 on v2

--- a/solution.py
+++ b/solution.py
@@ -142,19 +142,15 @@
 
     own = weights.astype(BF16)
     blocks = x.T.reshape(ys, ZS, rows, x.shape[0])
-    mine = lax.dynamic_index_in_dim(blocks, z, 1, False).reshape(ys * rows, x.shape[0])
     theirs = lax.dynamic_index_in_dim(blocks, 1 - z, 1, False).reshape(ys * rows, x.shape[0])
     leaving = theirs
     theirs = step(leaving, 0, 1)
+    mine = lax.dynamic_index_in_dim(after(blocks, theirs), z, 1, False).reshape(ys * rows, x.shape[0])
 
     reps = lax.axis_size("rep")
     width = anchor.shape[1]
     sent = after(drift[0], leaving).T.reshape(reps, width, rows)
     drifts = lax.all_to_all(sent, "rep", split_axis=0, concat_axis=0, tiled=True)
-    delta = jnp.sum(drifts.astype(F32), axis=0) / reps
-    momentum_new = 0.9 * momentum.T + delta
-    anchor_new = anchor.T - 0.7 * (delta + 0.9 * momentum_new)
-    copies = jnp.broadcast_to(anchor_new.astype(BF16)[None], (reps, width, rows))
 
     ups, downs = [step(own, 1)], [step(own, -1)]
     for n in range(half - 2):
@@ -163,11 +159,15 @@
     ups.append(step(after(ups[-1], theirs), 1))
     chunks = [own] + ups + downs
     where = jnp.stack([at(0)] + [at(-1 - n) for n in range(half)] + [at(1 + n) for n in range(half - 1)])
-    where, copies = lax.optimization_barrier((where, copies))
 
     cols = weights.shape[1] // 2
     own1, out1 = product(0, cols, where, mine, theirs, chunks)
     in1 = step(out1, 0, 1)
+    drifts = after(drifts, out1)
+    delta = jnp.sum(drifts.astype(F32), axis=0) / reps
+    momentum_new = 0.9 * momentum.T + delta
+    anchor_new = anchor.T - 0.7 * (delta + 0.9 * momentum_new)
+    copies = jnp.broadcast_to(anchor_new.astype(BF16)[None], (reps, width, rows))
     own2, out2 = product(cols, cols, where, mine, theirs, chunks)
     in2 = step(out2, 0, 1)
     keys1, slopes1 = norm(0, own1, in1, cotangent[0])

time: 169 us -> 167 us (0.988)
  starting transfers between devices: 108 us -> 94.1 us
  local copies, waits for them, and re-layouts: 8.68 us -> 14.4 us
  waiting for transfers between devices: 33.6 us -> 38.1 us
  Pallas kernels: 7.86 us -> 10.4 us
    all_to_all x1, starting transfers between devices: 24.2 us -> 7.16 us  [shards(): lax.all_to_all(copies, 'rep', split_axis=0, concat_axis=0, tiled=True)]
    ppermute x19, waiting for transfers between devices: 25.2 us -> 38.1 us  [step(): return lax.ppermute(value, 'fsdp', pairs)]
    all_to_all x1, waiting for transfers between devices: 8.37 us -> 0.01 us  [shards(): lax.all_to_all(sent, 'rep', split_axis=0, concat_axis=0, tiled=True)]
    unnamed x36 -> x54, local copies, waits for them, and re-layouts: 5.23 us -> 9.89 us
    ppermute x19, starting transfers between devices: 76 us -> 79.2 us  [step(): return lax.ppermute(value, 'fsdp', pairs)]
  transfers between devices with their start and end apart: 21 -> 21, of which waited for: 8 -> 7; matrix products, arithmetic and copies ran while one was open for 7% -> 7% of each run, Pallas kernels for 4% -> 6%
where the time goes in v3:
time: 167 us; the launch traced here: 166 us
  starting transfers between devices  94.1 us (56%)
  waiting for transfers between devices  38.1 us (23%)
  local copies, waits for them, and re-layouts  14.4 us (9%)
  Pallas kernels  10.4 us (6%)
  other arithmetic  7.4 us (4%)
    ppermute x19, starting transfers between devices, step(): return lax.ppermute(value, 'fsdp', pairs)  79.2 us
    ppermute x19, waiting for transfers between devices, step(): return lax.ppermute(value, 'fsdp', pairs)  38.1 us
    unnamed x54, local copies, waits for them, and re-layouts  9.89 us
    all_to_all x1, starting transfers between devices, shards(): lax.all_to_all(sent, 'rep', split_axis=0, concat_axis=0, tiled=True)  7.78 us
    all_to_all x1, starting transfers between devices, shards(): lax.all_to_all(copies, 'rep', split_axis=0, concat_axis=0, tiled=True)  7.16 us
    pallas_call x2, Pallas kernels, product(): pl.pallas_call(functools.partial(product_body, first), out_shape=(jax.Sha...  4.62 us
    pallas_call x2, Pallas kernels, partials(): pl.pallas_call(functools.partial(partial_body, len(slopes), rows), out_sh...  3.35 us
  transfers between devices with their start and end apart: 21, of which 7 were waited for; matrix products, arithmetic and copies ran while one was open for 7% of the time, Pallas kernels for 6%

profile of v3, /device:TPU:2, one launch (start us, length us, event | category | flops | bytes accessed | tf_op | source)
XLA Modules:
  0.0 165.8 jit_solution(7822958131949253363)
XLA Ops:
  1.7 3.5 %collective-permute-start.1 = (bf16[144,1024]{1,0:T(8,128)(2,1)S(1)}, bf16[144,1024]{1,0:T(8,128)(2,1)S(1)}, u32[]{:S(2)}, u32[]{:S(2)}) collective-permute-start(bf16[144,1024]{1,0:T(8,128)(2,1)S(1)} %bitcast_convert_fusion.refs_0_), channel_id=1, source_target_pairs={{0,2},{1,3},{2,4},{3,5},{4,6},{5,7},{6,8},{7,9},{8,10},{9,11},{10,... | collective-permute-start | bytes 884744 | tf_op jit(solution)/shard_map/ppermute | solution.py:138
  5.2 3.8 %collective-permute-start.5 = (bf16[144,1024]{1,0:T(8,128)(2,1)S(1)}, bf16[144,1024]{1,0:T(8,128)(2,1)S(1)}, u32[]{:S(2)}, u32[]{:S(2)}) collective-permute-start(bf16[144,1024]{1,0:T(8,128)(2,1)S(1)} %bitcast_convert_fusion.refs_0_), channel_id=1, source_target_pairs={{0,14},{1,15},{2,0},{3,1},{4,2},{5,3},{6,4},{7,5},{8,6},{9,7},{10,... | collective-permute-start | bytes 884744 | tf_op jit(solution)/shard_map/ppermute | solution.py:138
  11.9 10.9 %collective-permute-start = (bf16[1152,256]{1,0:T(8,128)(2,1)}, bf16[1152,256]{1,0:T(8,128)(2,1)S(1)}, u32[]{:S(2)}, u32[]{:S(2)}) collective-permute-start(bf16[1152,256]{1,0:T(8,128)(2,1)} %bitcast.5), channel_id=1, source_target_pairs={{0,1},{1,0},{2,3},{3,2},{4,5},{5,4},{6,7},{7,6},{8,9},{9,8},{10,11... | collective-permute-start | bytes 1769480 | tf_op jit(solution)/shard_map/ppermute | solution.py:138
  22.8 2.0 %collective-permute-start.2 = (bf16[144,1024]{1,0:T(8,128)(2,1)S(1)}, bf16[144,1024]{1,0:T(8,128)(2,1)S(1)}, u32[]{:S(2)}, u32[]{:S(2)}) collective-permute-start(bf16[144,1024]{1,0:T(8,128)(2,1)S(1)} %collective-permute-done.1.refs_1_), channel_id=1, source_target_pairs={{0,2},{1,3},{2,4},{3,5},{4,6},{5,7},{6,8},{7,9},{8,10},{9,11},{10,... | collective-permute-start | bytes 884744 | tf_op jit(solution)/shard_map/ppermute | solution.py:138
  24.9 5.0 %collective-permute-start.6 = (bf16[144,1024]{1,0:T(8,128)(2,1)S(1)}, bf16[144,1024]{1,0:T(8,128)(2,1)S(1)}, u32[]{:S(2)}, u32[]{:S(2)}) collective-permute-start(bf16[144,1024]{1,0:T(8,128)(2,1)S(1)} %collective-permute-done.5.refs_5_), channel_id=1, source_target_pairs={{0,14},{1,15},{2,0},{3,1},{4,2},{5,3},{6,4},{7,5},{8,6},{9,7},{10,... | collective-permute-start | bytes 884744 | tf_op jit(solution)/shard_map/ppermute | solution.py:138
  29.9 4.2 %collective-permute-done.2.refs_2_ = bf16[144,1024]{1,0:T(8,128)(2,1)S(1)} collective-permute-done((bf16[144,1024]{1,0:T(8,128)(2,1)S(1)}, bf16[144,1024]{1,0:T(8,128)(2,1)S(1)}, u32[]{:S(2)}, u32[]{:S(2)}) %collective-permute-start.2) | collective-permute-done | bytes 294944 | tf_op jit(solution)/shard_map/ppermute | solution.py:138
  34.1 1.9 %collective-permute-start.3 = (bf16[144,1024]{1,0:T(8,128)(2,1)S(1)}, bf16[144,1024]{1,0:T(8,128)(2,1)S(1)}, u32[]{:S(2)}, u32[]{:S(2)}) collective-permute-start(bf16[144,1024]{1,0:T(8,128)(2,1)S(1)} %collective-permute-done.2.refs_2_), channel_id=1, source_target_pairs={{0,2},{1,3},{2,4},{3,5},{4,6},{5,7},{6,8},{7,9},{8,10},{9,11},{10,... | collective-permute-start | bytes 884744 | tf_op jit(solution)/shard_map/ppermute | solution.py:138
  37.1 7.8 %all-to-all-start = ((bf16[32,32,144]{2,1,0:T(8,128)(2,1)}), bf16[32,32,144]{2,1,0:T(8,128)(2,1)}, u32[]{:S(2)}, u32[]{:S(2)}) async-start(bf16[32,32,144]{2,1,0:T(8,128)(2,1)} %bitcast.7), calls=%async_computation | async-start | bytes 1048576 | tf_op jit(solution)/shard_map/all_to_all | solution.py:153
  44.8 5.1 %collective-permute-start.7 = (bf16[144,1024]{1,0:T(8,128)(2,1)S(1)}, bf16[144,1024]{1,0:T(8,128)(2,1)S(1)}, u32[]{:S(2)}, u32[]{:S(2)}) collective-permute-start(bf16[144,1024]{1,0:T(8,128)(2,1)S(1)} %collective-permute-done.6.refs_6_), channel_id=1, source_target_pairs={{0,14},{1,15},{2,0},{3,1},{4,2},{5,3},{6,4},{7,5},{8,6},{9,7},{10,... | collective-permute-start | bytes 884744 | tf_op jit(solution)/shard_map/ppermute | solution.py:138
  50.0 1.9 %collective-permute-start.4 = (bf16[144,1024]{1,0:T(8,128)(2,1)S(1)}, bf16[144,1024]{1,0:T(8,128)(2,1)}, u32[]{:S(2)}, u32[]{:S(2)}) collective-permute-start(bf16[144,1024]{1,0:T(8,128)(2,1)S(1)} %collective-permute-done.3.refs_3_), channel_id=1, source_target_pairs={{0,2},{1,3},{2,4},{3,5},{4,6},{5,7},{6,8},{7,9},{8,10},{9,11},{10,... | collective-permute-start | bytes 884744 | tf_op jit(solution)/shard_map/ppermute | solution.py:138
  53.3 3.3 %collective-permute-done.7.refs_7_ = bf16[144,1024]{1,0:T(8,128)(2,1)S(1)} collective-permute-done((bf16[144,1024]{1,0:T(8,128)(2,1)S(1)}, bf16[144,1024]{1,0:T(8,128)(2,1)S(1)}, u32[]{:S(2)}, u32[]{:S(2)}) %collective-permute-start.7) | collective-permute-done | bytes 294944 | tf_op jit(solution)/shard_map/ppermute | solution.py:138
  56.5 5.5 %collective-permute-done.4.refs_4_ = bf16[144,1024]{1,0:T(8,128)(2,1)} collective-permute-done((bf16[144,1024]{1,0:T(8,128)(2,1)S(1)}, bf16[144,1024]{1,0:T(8,128)(2,1)}, u32[]{:S(2)}, u32[]{:S(2)}) %collective-permute-start.4) | collective-permute-done | bytes 294944 | tf_op jit(solution)/shard_map/ppermute | solution.py:138
  62.0 2.3 %product.3 = (f32[256,512]{1,0:T(8,128)S(1)}, bf16[256,512]{1,0:T(8,128)(2,1)}) custom-call(s32[8]{0:T(128)S(1)} %stack.51.ids, bf16[1152,256]{1,0:T(8,128)(2,1)S(1)} %bitcast.67, bf16[1152,256]{1,0:T(8,128)(2,1)S(1)} %collective-permute-done.theirs_ref, bf16[144,1024]{1,0:T(8,128)(2,1)S(1)} %bitcast_convert_fusion.refs_0_, ...), custom_call_target="tpu_custom_call" | custom-call | flops 603979776 | bytes 4194304 | tf_op jit(solution)/shard_map/product/pallas_call | solution.py:40
  65.1 4.6 %collective-permute-start.9 = (bf16[256,512]{1,0:T(8,128)(2,1)}, bf16[256,512]{1,0:T(8,128)(2,1)}, u32[]{:S(2)}, u32[]{:S(2)}) collective-permute-start(bf16[256,512]{1,0:T(8,128)(2,1)} %get-tuple-element.39), channel_id=1, source_target_pairs={{0,1},{1,0},{2,3},{3,2},{4,5},{5,4},{6,7},{7,6},{8,9},{9,8},{10,11... | collective-permute-start | bytes 786440 | tf_op jit(solution)/shard_map/ppermute | solution.py:138
  70.6 2.3 %product.2 = (f32[256,512]{1,0:T(8,128)S(1)}, bf16[256,512]{1,0:T(8,128)(2,1)}) custom-call(s32[8]{0:T(128)S(1)} %stack.51.ids, bf16[1152,256]{1,0:T(8,128)(2,1)S(1)} %bitcast.68, bf16[1152,256]{1,0:T(8,128)(2,1)S(1)} %collective-permute-done.theirs_ref, bf16[144,1024]{1,0:T(8,128)(2,1)S(1)} %bitcast_convert_fusion.refs_0_, ...), custom_call_target="tpu_custom_call" | custom-call | flops 603979776 | bytes 4194304 | tf_op jit(solution)/shard_map/product/pallas_call | solution.py:40
  73.7 5.4 %collective-permute-start.8 = (bf16[256,512]{1,0:T(8,128)(2,1)}, bf16[256,512]{1,0:T(8,128)(2,1)S(1)}, u32[]{:S(2)}, u32[]{:S(2)}) collective-permute-start(bf16[256,512]{1,0:T(8,128)(2,1)} %get-tuple-element.33), channel_id=1, source_target_pairs={{0,1},{1,0},{2,3},{3,2},{4,5},{5,4},{6,7},{7,6},{8,9},{9,8},{10,11... | collective-permute-start | bytes 786440 | tf_op jit(solution)/shard_map/ppermute | solution.py:138
  83.6 4.4 %collective-permute-start.11 = (bf16[256,512]{1,0:T(8,128)(2,1)S(1)}, bf16[256,512]{1,0:T(8,128)(2,1)S(1)}, u32[]{:S(2)}, u32[]{:S(2)}) collective-permute-start(bf16[256,512]{1,0:T(8,128)(2,1)S(1)} %get-tuple-element.40.refs_1_), channel_id=1, source_target_pairs={{0,1},{1,0},{2,3},{3,2},{4,5},{5,4},{6,7},{7,6},{8,9},{9,8},{10,11... | collective-permute-start | bytes 786440 | tf_op jit(solution)/shard_map/ppermute | solution.py:138
  88.1 8.3 %collective-permute-done.8.other_ref = bf16[256,512]{1,0:T(8,128)(2,1)S(1)} collective-permute-done((bf16[256,512]{1,0:T(8,128)(2,1)}, bf16[256,512]{1,0:T(8,128)(2,1)S(1)}, u32[]{:S(2)}, u32[]{:S(2)}) %collective-permute-start.8) | collective-permute-done | bytes 262176 | tf_op jit(solution)/shard_map/ppermute | solution.py:138
  97.7 7.2 %collective-permute-start.10 = (bf16[256,512]{1,0:T(8,128)(2,1)S(1)}, bf16[256,512]{1,0:T(8,128)(2,1)S(1)}, u32[]{:S(2)}, u32[]{:S(2)}) collective-permute-start(bf16[256,512]{1,0:T(8,128)(2,1)S(1)} %get-tuple-element.37.refs_0_), channel_id=1, source_target_pairs={{0,1},{1,0},{2,3},{3,2},{4,5},{5,4},{6,7},{7,6},{8,9},{9,8},{10,11... | collective-permute-start | bytes 786440 | tf_op jit(solution)/shard_map/ppermute | solution.py:138
  105.8 7.2 %all-to-all-start.1 = ((bf16[32,32,144]{2,1,0:T(8,128)(2,1)}), bf16[32,32,144]{2,1,0:T(8,128)(2,1)}, u32[]{:S(2)}, u32[]{:S(2)}) async-start(bf16[32,32,144]{2,1,0:T(8,128)(2,1)} %broadcast_in_dim.12), calls=%async_computation.1 | async-start | bytes 1048576 | tf_op jit(solution)/shard_map/all_to_all | solution.py:179
  113.1 7.9 %collective-permute-done.10.refs_2_ = bf16[256,512]{1,0:T(8,128)(2,1)S(1)} collective-permute-done((bf16[256,512]{1,0:T(8,128)(2,1)S(1)}, bf16[256,512]{1,0:T(8,128)(2,1)S(1)}, u32[]{:S(2)}, u32[]{:S(2)}) %collective-permute-start.10) | collective-permute-done | bytes 262176 | tf_op jit(solution)/shard_map/ppermute | solution.py:138
  121.0 1.7 %partials.3 = (bf16[144,1024]{1,0:T(8,128)(2,1)}, bf16[144,1024]{1,0:T(8,128)(2,1)}) custom-call(s32[2]{0:T(128)S(1)} %pad_add_fusion.ids, bf16[1152,256]{1,0:T(8,128)(2,1)S(1)} %bitcast.69, bf16[1152,256]{1,0:T(8,128)(2,1)S(1)} %collective-permute-done.theirs_ref, bf16[256,512]{1,0:T(8,128)(2,1)S(1)} %get-tuple-element.37.refs_0_, ...), custom_call_target="tpu_custom_call" | custom-call | flops 301989888 | bytes 2686976 | tf_op jit(solution)/shard_map/partials/pallas_call | solution.py:91
  122.7 3.3 %collective-permute-start.12 = (bf16[144,1024]{1,0:T(8,128)(2,1)}, bf16[144,1024]{1,0:T(8,128)(2,1)S(1)}, u32[]{:S(2)}, u32[]{:S(2)}) collective-permute-start(bf16[144,1024]{1,0:T(8,128)(2,1)} %get-tuple-element.46), channel_id=1, source_target_pairs={{0,2},{1,3},{2,4},{3,5},{4,6},{5,7},{6,8},{7,9},{8,10},{9,11},{10,... | collective-permute-start | bytes 884744 | tf_op jit(solution)/shard_map/ppermute | solution.py:138
  126.1 3.7 %collective-permute-start.16 = (bf16[144,1024]{1,0:T(8,128)(2,1)}, bf16[144,1024]{1,0:T(8,128)(2,1)S(1)}, u32[]{:S(2)}, u32[]{:S(2)}) collective-permute-start(bf16[144,1024]{1,0:T(8,128)(2,1)} %get-tuple-element.49), channel_id=1, source_target_pairs={{0,14},{1,15},{2,0},{3,1},{4,2},{5,3},{6,4},{7,5},{8,6},{9,7},{10,... | collective-permute-start | bytes 884744 | tf_op jit(solution)/shard_map/ppermute | solution.py:138
  133.5 2.1 %collective-permute-start.13 = (bf16[144,1024]{1,0:T(8,128)(2,1)S(1)}, bf16[144,1024]{1,0:T(8,128)(2,1)S(1)}, u32[]{:S(2)}, u32[]{:S(2)}) collective-permute-start(bf16[144,1024]{1,0:T(8,128)(2,1)S(1)} %add.220), channel_id=1, source_target_pairs={{0,2},{1,3},{2,4},{3,5},{4,6},{5,7},{6,8},{7,9},{8,10},{9,11},{10,... | collective-permute-start | bytes 884744 | tf_op jit(solution)/shard_map/ppermute | solution.py:138
  135.7 4.9 %collective-permute-start.17 = (bf16[144,1024]{1,0:T(8,128)(2,1)S(1)}, bf16[144,1024]{1,0:T(8,128)(2,1)S(1)}, u32[]{:S(2)}, u32[]{:S(2)}) collective-permute-start(bf16[144,1024]{1,0:T(8,128)(2,1)S(1)} %add.223), channel_id=1, source_target_pairs={{0,14},{1,15},{2,0},{3,1},{4,2},{5,3},{6,4},{7,5},{8,6},{9,7},{10,... | collective-permute-start | bytes 884744 | tf_op jit(solution)/shard_map/ppermute | solution.py:138
  140.7 2.2 %convert_multiply_fusion = f32[32,32,144]{2,1,0:T(8,128)} fusion(bf16[32,32,144]{2,1,0:T(8,128)(2,1)} %all-to-all-done.1), kind=kLoop, calls=%fused_computation | loop fusion | flops 294912 | bytes 884736 | tf_op jit(solution)/shard_map/mul | solution.py:187
  144.5 2.1 %collective-permute-start.14 = (bf16[144,1024]{1,0:T(8,128)(2,1)S(1)}, bf16[144,1024]{1,0:T(8,128)(2,1)S(1)}, u32[]{:S(2)}, u32[]{:S(2)}) collective-permute-start(bf16[144,1024]{1,0:T(8,128)(2,1)S(1)} %add.221), channel_id=1, source_target_pairs={{0,2},{1,3},{2,4},{3,5},{4,6},{5,7},{6,8},{7,9},{8,10},{9,11},{10,... | collective-permute-start | bytes 884744 | tf_op jit(solution)/shard_map/ppermute | solution.py:138
  146.7 5.3 %collective-permute-start.18 = (bf16[144,1024]{1,0:T(8,128)(2,1)S(1)}, bf16[144,1024]{1,0:T(8,128)(2,1)S(1)}, u32[]{:S(2)}, u32[]{:S(2)}) collective-permute-start(bf16[144,1024]{1,0:T(8,128)(2,1)S(1)} %add.224), channel_id=1, source_target_pairs={{0,14},{1,15},{2,0},{3,1},{4,2},{5,3},{6,4},{7,5},{8,6},{9,7},{10,... | collective-permute-start | bytes 884744 | tf_op jit(solution)/shard_map/ppermute | solution.py:138
  152.0 2.5 %collective-permute-done.14.refs_1_ = bf16[144,1024]{1,0:T(8,128)(2,1)S(1)} collective-permute-done((bf16[144,1024]{1,0:T(8,128)(2,1)S(1)}, bf16[144,1024]{1,0:T(8,128)(2,1)S(1)}, u32[]{:S(2)}, u32[]{:S(2)}) %collective-permute-start.14) | collective-permute-done | bytes 294944 | tf_op jit(solution)/shard_map/ppermute | solution.py:138
  154.5 1.9 %collective-permute-start.15 = (bf16[144,1024]{1,0:T(8,128)(2,1)S(1)}, bf16[144,1024]{1,0:T(8,128)(2,1)S(1)}, u32[]{:S(2)}, u32[]{:S(2)}) collective-permute-start(bf16[144,1024]{1,0:T(8,128)(2,1)S(1)} %add.222), channel_id=1, source_target_pairs={{0,2},{1,3},{2,4},{3,5},{4,6},{5,7},{6,8},{7,9},{8,10},{9,11},{10,... | collective-permute-start | bytes 884744 | tf_op jit(solution)/shard_map/ppermute | solution.py:138
  158.0 6.4 %collective-permute-done.15 = bf16[144,1024]{1,0:T(8,128)(2,1)S(1)} collective-permute-done((bf16[144,1024]{1,0:T(8,128)(2,1)S(1)}, bf16[144,1024]{1,0:T(8,128)(2,1)S(1)}, u32[]{:S(2)}, u32[]{:S(2)}) %collective-permute-start.15) | collective-permute-done | bytes 294944 | tf_op jit(solution)/shard_map/ppermute | solution.py:138
  (89 shorter events, 23.7 us)
Async XLA Ops:
  1.7 21.1 %collective-permute-start.1 = (bf16[144,1024]{1,0:T(8,128)(2,1)S(1)}, bf16[144,1024]{1,0:T(8,128)(2,1)S(1)}, u32[]{:S(2)}, u32[]{:S(2)}) collective-permute-start(bf16[144,1024]{1,0:T(8,128)(2,1)S(1)} %bitcast_convert_fusion.refs_0_), channel_id=1, source_target_pairs={{0,2},{1,3},{2,4},{3,5},{4,6},{5,7},{6,8},{7,9},{8,10},{9,11},{10,... | collective-permute-start | bytes 884744 | tf_op jit(solution)/shard_map/ppermute | solution.py:138
  5.2 19.6 %collective-permute-start.5 = (bf16[144,1024]{1,0:T(8,128)(2,1)S(1)}, bf16[144,1024]{1,0:T(8,128)(2,1)S(1)}, u32[]{:S(2)}, u32[]{:S(2)}) collective-permute-start(bf16[144,1024]{1,0:T(8,128)(2,1)S(1)} %bitcast_convert_fusion.refs_0_), channel_id=1, source_target_pairs={{0,14},{1,15},{2,0},{3,1},{4,2},{5,3},{6,4},{7,5},{8,6},{9,7},{10,... | collective-permute-start | bytes 884744 | tf_op jit(solution)/shard_map/ppermute | solution.py:138
  10.7 25.4 %copy-start.19 = (bf16[1,144,1024]{2,1,0:T(8,128)(2,1)S(1)}, bf16[1,144,1024]{2,1,0:T(8,128)(2,1)}, u32[]{:S(2)}) copy-start(bf16[1,144,1024]{2,1,0:T(8,128)(2,1)} %param.13) | copy-start | bytes 884740
  11.9 38.1 %collective-permute-start = (bf16[1152,256]{1,0:T(8,128)(2,1)}, bf16[1152,256]{1,0:T(8,128)(2,1)S(1)}, u32[]{:S(2)}, u32[]{:S(2)}) collective-permute-start(bf16[1152,256]{1,0:T(8,128)(2,1)} %bitcast.5), channel_id=1, source_target_pairs={{0,1},{1,0},{2,3},{3,2},{4,5},{5,4},{6,7},{7,6},{8,9},{9,8},{10,11... | collective-permute-start | bytes 1769480 | tf_op jit(solution)/shard_map/ppermute | solution.py:138
  22.8 11.3 %collective-permute-start.2 = (bf16[144,1024]{1,0:T(8,128)(2,1)S(1)}, bf16[144,1024]{1,0:T(8,128)(2,1)S(1)}, u32[]{:S(2)}, u32[]{:S(2)}) collective-permute-start(bf16[144,1024]{1,0:T(8,128)(2,1)S(1)} %collective-permute-done.1.refs_1_), channel_id=1, source_target_pairs={{0,2},{1,3},{2,4},{3,5},{4,6},{5,7},{6,8},{7,9},{8,10},{9,11},{10,... | collective-permute-start | bytes 884744 | tf_op jit(solution)/shard_map/ppermute | solution.py:138
  24.9 20.0 %collective-permute-start.6 = (bf16[144,1024]{1,0:T(8,128)(2,1)S(1)}, bf16[144,1024]{1,0:T(8,128)(2,1)S(1)}, u32[]{:S(2)}, u32[]{:S(2)}) collective-permute-start(bf16[144,1024]{1,0:T(8,128)(2,1)S(1)} %collective-permute-done.5.refs_5_), channel_id=1, source_target_pairs={{0,14},{1,15},{2,0},{3,1},{4,2},{5,3},{6,4},{7,5},{8,6},{9,7},{10,... | collective-permute-start | bytes 884744 | tf_op jit(solution)/shard_map/ppermute | solution.py:138
  34.1 15.9 %collective-permute-start.3 = (bf16[144,1024]{1,0:T(8,128)(2,1)S(1)}, bf16[144,1024]{1,0:T(8,128)(2,1)S(1)}, u32[]{:S(2)}, u32[]{:S(2)}) collective-permute-start(bf16[144,1024]{1,0:T(8,128)(2,1)S(1)} %collective-permute-done.2.refs_2_), channel_id=1, source_target_pairs={{0,2},{1,3},{2,4},{3,5},{4,6},{5,7},{6,8},{7,9},{8,10},{9,11},{10,... | collective-permute-start | bytes 884744 | tf_op jit(solution)/shard_map/ppermute | solution.py:138
  37.1 42.1 %all-to-all-start = ((bf16[32,32,144]{2,1,0:T(8,128)(2,1)}), bf16[32,32,144]{2,1,0:T(8,128)(2,1)}, u32[]{:S(2)}, u32[]{:S(2)}) async-start(bf16[32,32,144]{2,1,0:T(8,128)(2,1)} %bitcast.7), calls=%async_computation | async-start | bytes 1048576 | tf_op jit(solution)/shard_map/all_to_all | solution.py:153
  44.8 11.7 %collective-permute-start.7 = (bf16[144,1024]{1,0:T(8,128)(2,1)S(1)}, bf16[144,1024]{1,0:T(8,128)(2,1)S(1)}, u32[]{:S(2)}, u32[]{:S(2)}) collective-permute-start(bf16[144,1024]{1,0:T(8,128)(2,1)S(1)} %collective-permute-done.6.refs_6_), channel_id=1, source_target_pairs={{0,14},{1,15},{2,0},{3,1},{4,2},{5,3},{6,4},{7,5},{8,6},{9,7},{10,... | collective-permute-start | bytes 884744 | tf_op jit(solution)/shard_map/ppermute | solution.py:138
  50.0 12.0 %collective-permute-start.4 = (bf16[144,1024]{1,0:T(8,128)(2,1)S(1)}, bf16[144,1024]{1,0:T(8,128)(2,1)}, u32[]{:S(2)}, u32[]{:S(2)}) collective-permute-start(bf16[144,1024]{1,0:T(8,128)(2,1)S(1)} %collective-permute-done.3.refs_3_), channel_id=1, source_target_pairs={{0,2},{1,3},{2,4},{3,5},{4,6},{5,7},{6,8},{7,9},{8,10},{9,11},{10,... | collective-permute-start | bytes 884744 | tf_op jit(solution)/shard_map/ppermute | solution.py:138
  65.1 15.3 %copy-start = (bf16[1,256,1024]{2,1,0:T(8,128)(2,1)S(1)}, bf16[1,256,1024]{2,1,0:T(8,128)(2,1)}, u32[]{:S(2)}) copy-start(bf16[1,256,1024]{2,1,0:T(8,128)(2,1)} %param.9) | copy-start | bytes 1572868
  65.1 15.2 %collective-permute-start.9 = (bf16[256,512]{1,0:T(8,128)(2,1)}, bf16[256,512]{1,0:T(8,128)(2,1)}, u32[]{:S(2)}, u32[]{:S(2)}) collective-permute-start(bf16[256,512]{1,0:T(8,128)(2,1)} %get-tuple-element.39), channel_id=1, source_target_pairs={{0,1},{1,0},{2,3},{3,2},{4,5},{5,4},{6,7},{7,6},{8,9},{9,8},{10,11... | collective-permute-start | bytes 786440 | tf_op jit(solution)/shard_map/ppermute | solution.py:138
  73.7 22.6 %copy-start.4 = (f32[256,512]{1,0:T(8,128)S(1)}, f32[256,512]{1,0:T(8,128)}, u32[]{:S(2)}) copy-start(f32[256,512]{1,0:T(8,128)} %copy-done.3) | copy-start | bytes 1572868
  73.7 22.6 %collective-permute-start.8 = (bf16[256,512]{1,0:T(8,128)(2,1)}, bf16[256,512]{1,0:T(8,128)(2,1)S(1)}, u32[]{:S(2)}, u32[]{:S(2)}) collective-permute-start(bf16[256,512]{1,0:T(8,128)(2,1)} %get-tuple-element.33), channel_id=1, source_target_pairs={{0,1},{1,0},{2,3},{3,2},{4,5},{5,4},{6,7},{7,6},{8,9},{9,8},{10,11... | collective-permute-start | bytes 786440 | tf_op jit(solution)/shard_map/ppermute | solution.py:138
  80.3 24.6 %copy-start.20 = (f32[32,144]{1,0:T(8,128)}, f32[32,144]{1,0:T(8,128)S(1)}, u32[]{:S(2)}) copy-start(f32[32,144]{1,0:T(8,128)S(1)} %convert_reduce_fusion) | copy-start | bytes 55300
  81.4 23.5 %copy-start.22 = (f32[144,32]{0,1:T(8,128)S(1)}, f32[144,32]{0,1:T(8,128)}, u32[]{:S(2)}) copy-start(f32[144,32]{0,1:T(8,128)} %param.14) | copy-start | bytes 55300
  81.4 23.5 %copy-start.24 = (f32[144,32]{0,1:T(8,128)S(1)}, f32[144,32]{0,1:T(8,128)}, u32[]{:S(2)}) copy-start(f32[144,32]{0,1:T(8,128)} %param.15) | copy-start | bytes 55300
  83.6 29.5 %collective-permute-start.11 = (bf16[256,512]{1,0:T(8,128)(2,1)S(1)}, bf16[256,512]{1,0:T(8,128)(2,1)S(1)}, u32[]{:S(2)}, u32[]{:S(2)}) collective-permute-start(bf16[256,512]{1,0:T(8,128)(2,1)S(1)} %get-tuple-element.40.refs_1_), channel_id=1, source_target_pairs={{0,1},{1,0},{2,3},{3,2},{4,5},{5,4},{6,7},{7,6},{8,9},{9,8},{10,11... | collective-permute-start | bytes 786440 | tf_op jit(solution)/shard_map/ppermute | solution.py:138
  97.7 25.1 %copy-start.7 = (bf16[256,512]{1,0:T(8,128)(2,1)}, bf16[256,512]{1,0:T(8,128)(2,1)S(1)}, u32[]{:S(2)}) copy-start(bf16[256,512]{1,0:T(8,128)(2,1)S(1)} %get-tuple-element.37.refs_0_) | copy-start | bytes 786436
  97.7 23.3 %collective-permute-start.10 = (bf16[256,512]{1,0:T(8,128)(2,1)S(1)}, bf16[256,512]{1,0:T(8,128)(2,1)S(1)}, u32[]{:S(2)}, u32[]{:S(2)}) collective-permute-start(bf16[256,512]{1,0:T(8,128)(2,1)S(1)} %get-tuple-element.37.refs_0_), channel_id=1, source_target_pairs={{0,1},{1,0},{2,3},{3,2},{4,5},{5,4},{6,7},{7,6},{8,9},{9,8},{10,11... | collective-permute-start | bytes 786440 | tf_op jit(solution)/shard_map/ppermute | solution.py:138
  105.8 34.9 %all-to-all-start.1 = ((bf16[32,32,144]{2,1,0:T(8,128)(2,1)}), bf16[32,32,144]{2,1,0:T(8,128)(2,1)}, u32[]{:S(2)}, u32[]{:S(2)}) async-start(bf16[32,32,144]{2,1,0:T(8,128)(2,1)} %broadcast_in_dim.12), calls=%async_computation.1 | async-start | bytes 1048576 | tf_op jit(solution)/shard_map/all_to_all | solution.py:179
  122.7 10.7 %collective-permute-start.12 = (bf16[144,1024]{1,0:T(8,128)(2,1)}, bf16[144,1024]{1,0:T(8,128)(2,1)S(1)}, u32[]{:S(2)}, u32[]{:S(2)}) collective-permute-start(bf16[144,1024]{1,0:T(8,128)(2,1)} %get-tuple-element.46), channel_id=1, source_target_pairs={{0,2},{1,3},{2,4},{3,5},{4,6},{5,7},{6,8},{7,9},{8,10},{9,11},{10,... | collective-permute-start | bytes 884744 | tf_op jit(solution)/shard_map/ppermute | solution.py:138
  126.1 9.6 %collective-permute-start.16 = (bf16[144,1024]{1,0:T(8,128)(2,1)}, bf16[144,1024]{1,0:T(8,128)(2,1)S(1)}, u32[]{:S(2)}, u32[]{:S(2)}) collective-permute-start(bf16[144,1024]{1,0:T(8,128)(2,1)} %get-tuple-element.49), channel_id=1, source_target_pairs={{0,14},{1,15},{2,0},{3,1},{4,2},{5,3},{6,4},{7,5},{8,6},{9,7},{10,... | collective-permute-start | bytes 884744 | tf_op jit(solution)/shard_map/ppermute | solution.py:138
  133.5 10.9 %collective-permute-start.13 = (bf16[144,1024]{1,0:T(8,128)(2,1)S(1)}, bf16[144,1024]{1,0:T(8,128)(2,1)S(1)}, u32[]{:S(2)}, u32[]{:S(2)}) collective-permute-start(bf16[144,1024]{1,0:T(8,128)(2,1)S(1)} %add.220), channel_id=1, source_target_pairs={{0,2},{1,3},{2,4},{3,5},{4,6},{5,7},{6,8},{7,9},{8,10},{9,11},{10,... | collective-permute-start | bytes 884744 | tf_op jit(solution)/shard_map/ppermute | solution.py:138
  135.7 10.8 %collective-permute-start.17 = (bf16[144,1024]{1,0:T(8,128)(2,1)S(1)}, bf16[144,1024]{1,0:T(8,128)(2,1)S(1)}, u32[]{:S(2)}, u32[]{:S(2)}) collective-permute-start(bf16[144,1024]{1,0:T(8,128)(2,1)S(1)} %add.223), channel_id=1, source_target_pairs={{0,14},{1,15},{2,0},{3,1},{4,2},{5,3},{6,4},{7,5},{8,6},{9,7},{10,... | collective-permute-start | bytes 884744 | tf_op jit(solution)/shard_map/ppermute | solution.py:138
  144.5 12.6 %copy-start.12 = (bf16[256,512]{1,0:T(8,128)(2,1)S(1)}, bf16[256,512]{1,0:T(8,128)(2,1)}, u32[]{:S(2)}) copy-start(bf16[256,512]{1,0:T(8,128)(2,1)} %copy-done.11) | copy-start | bytes 786436
  144.5 10.0 %collective-permute-start.14 = (bf16[144,1024]{1,0:T(8,128)(2,1)S(1)}, bf16[144,1024]{1,0:T(8,128)(2,1)S(1)}, u32[]{:S(2)}, u32[]{:S(2)}) collective-permute-start(bf16[144,1024]{1,0:T(8,128)(2,1)S(1)} %add.221), channel_id=1, source_target_pairs={{0,2},{1,3},{2,4},{3,5},{4,6},{5,7},{6,8},{7,9},{8,10},{9,11},{10,... | collective-permute-start | bytes 884744 | tf_op jit(solution)/shard_map/ppermute | solution.py:138
  146.7 17.7 %copy-start.16 = (f32[1,144,1024]{2,1,0:T(8,128)S(1)}, f32[1,144,1024]{2,1,0:T(8,128)}, u32[]{:S(2)}) copy-start(f32[1,144,1024]{2,1,0:T(8,128)} %param.10) | copy-start | bytes 1769476
  146.7 17.7 %copy-start.17 = (f32[1,144,1024]{2,1,0:T(8,128)S(1)}, f32[1,144,1024]{2,1,0:T(8,128)}, u32[]{:S(2)}) copy-start(f32[1,144,1024]{2,1,0:T(8,128)} %param.12) | copy-start | bytes 1769476
  146.7 17.7 %copy-start.18 = (f32[1,144,1024]{2,1,0:T(8,128)S(1)}, f32[1,144,1024]{2,1,0:T(8,128)}, u32[]{:S(2)}) copy-start(f32[1,144,1024]{2,1,0:T(8,128)} %param.11) | copy-start | bytes 1769476
  146.7 11.3 %collective-permute-start.18 = (bf16[144,1024]{1,0:T(8,128)(2,1)S(1)}, bf16[144,1024]{1,0:T(8,128)(2,1)S(1)}, u32[]{:S(2)}, u32[]{:S(2)}) collective-permute-start(bf16[144,1024]{1,0:T(8,128)(2,1)S(1)} %add.224), channel_id=1, source_target_pairs={{0,14},{1,15},{2,0},{3,1},{4,2},{5,3},{6,4},{7,5},{8,6},{9,7},{10,... | collective-permute-start | bytes 884744 | tf_op jit(solution)/shard_map/ppermute | solution.py:138
  154.5 9.8 %collective-permute-start.15 = (bf16[144,1024]{1,0:T(8,128)(2,1)S(1)}, bf16[144,1024]{1,0:T(8,128)(2,1)S(1)}, u32[]{:S(2)}, u32[]{:S(2)}) collective-permute-start(bf16[144,1024]{1,0:T(8,128)(2,1)S(1)} %add.222), channel_id=1, source_target_pairs={{0,2},{1,3},{2,4},{3,5},{4,6},{5,7},{6,8},{7,9},{8,10},{9,11},{10,... | collective-permute-start | bytes 884744 | tf_op jit(solution)/shard_map/ppermute | solution.py:138
  (15 other events, 73.7 us)
